TPU v7x, 32 devices: a whole 2x2x4 slice. The times are simulated.
32 devices in a mesh: batch: 4 (over y, x), slab: 8 (over z, core).
Axes of the slice: x: 2, y: 2, z: 4, core: 2. Of those that a mesh axis runs over, the one named last changes fastest.
Arguments:
- activations: bfloat16 [4, 64, 8, 16, 128], P('batch', None, 'slab'), may hold values from -6 to 6
- grad_image: bfloat16 [4, 256, 256], P('batch', 'slab'), may hold values from -48 to 48
- pose_bin: int32 [4], P('batch'), may hold values from 0 to 31
- shift: int32 [4], P('batch'), may hold values from -8 to 8
- weight_a: bfloat16 [64, 2048], replicated, may hold values from -0.25 to 0.25
- bias_a: float32 [32], replicated, may hold values from -3 to 3
- weight_b: bfloat16 [32, 27], replicated, may hold values from -0.21875 to 0.21875
Outputs:
- grad_input: bfloat16 [4, 64, 8, 16, 128], P('batch', None, 'slab')
- grad_weight_a: float32 [64, 2048], replicated
- grad_bias_a: float32 [32], replicated
- grad_weight_b: float32 [32, 27], replicated
- grad_bias_b: float32 [1], replicated
All inputs are finite; a program needn't handle non-finite values.
Results may differ from a plain program's by a relative error of at most 0.005.
Values may be sent and summed in bfloat16 or wider, within the bound.
A program may use at most 192 MiB of HBM per device.

v0:
```python
import math

import jax
import jax.numpy as jnp
from jax import lax
from jax.sharding import PartitionSpec as P

NBINS = 32


forward_taps = (((0, 1), (-1, 3)), ((0, 2), (1, 0)))


def extended_2(array, sides, width):
    for axis, dim in sides:
        peers, length = (lax.axis_size(axis), array.shape[dim])
        up = [(i, (i + 1) % peers) for i in range(peers - 1)]
        down = [(j, i) for i, j in up]
        last = lax.slice_in_dim(array, length - width, length, axis=dim)
        initial = lax.slice_in_dim(array, 0, width, axis=dim)
        before = lax.ppermute(last, axis, up)
        after = lax.ppermute(initial, axis, down)
        array = jnp.concatenate([before, array, after], axis=dim)
    return array


def interp_weights(
    angle_bin,
    offset,
    plane_first,
    plane_count,
    row_count,
    total_depth,
    pixel_count,
    image_rows,
    bin_count,
):
    angle_value = (angle_bin.astype(jnp.float32) + 0.5) * (math.pi / bin_count)
    plane_pos = (plane_first + jnp.arange(plane_count, dtype=jnp.int32)).astype(jnp.float32)
    row_pos = jnp.arange(row_count, dtype=jnp.float32)
    center = (
        (row_pos[None, :] - 0.5 * (row_count - 1)) * jnp.cos(angle_value)
        + (plane_pos[:, None] - 0.5 * (total_depth - 1)) * jnp.sin(angle_value)
        + (0.5 * (image_rows - 1) + offset.astype(jnp.float32))
    )
    pixels = jnp.arange(pixel_count, dtype=jnp.int32).astype(jnp.float32)
    return jnp.maximum(1.0 - jnp.abs(pixels[None, :] - center.reshape(-1, 1)), 0.0)


def transposed_forward(padded_in, weight_a, bias_a, firsts, count):
    chan_in = padded_in.shape[0]
    coarse_y = padded_in.shape[2] - 2
    coarse_x = padded_in.shape[3] - 2
    chan_out = bias_a.shape[0]
    parity_parts = []
    for par_z in range(2):
        row_parts = []
        for par_y in range(2):
            col_parts = []
            for par_x in range(2):
                running = jnp.zeros((chan_out, count * coarse_y * coarse_x), jnp.float32)
                for off_z, tap_z in forward_taps[par_z]:
                    for off_y, tap_y in forward_taps[par_y]:
                        for off_x, tap_x in forward_taps[par_x]:
                            start_z = firsts[par_z] + 1 + off_z
                            block = padded_in[
                                :,
                                start_z : start_z + count,
                                1 + off_y : 1 + off_y + coarse_y,
                                1 + off_x : 1 + off_x + coarse_x,
                            ].reshape(chan_in, -1)
                            tap_index = tap_z * 16 + tap_y * 4 + tap_x
                            matrix = weight_a[:, tap_index * chan_out : (tap_index + 1) * chan_out]
                            running = running + jnp.dot(
                                matrix.T, block, preferred_element_type=jnp.float32
                            )
                col_parts.append(running.reshape(chan_out, count, coarse_y, coarse_x))
            row_parts.append(jnp.stack(col_parts, axis=-1))
        parity_parts.append(jnp.stack(row_parts, axis=3))
    ordered = [parity_parts[0], parity_parts[1]]
    joined = jnp.stack(ordered, axis=2).reshape(chan_out, 2 * count, 2 * coarse_y, 2 * coarse_x)
    return joined + bias_a[:, None, None, None]


def shifted_stack(padded_grad, planes, row_count, col_count):
    layers = []
    for tap_z in range(3):
        for tap_y in range(3):
            for tap_x in range(3):
                layers.append(
                    padded_grad[
                        tap_z : tap_z + planes, tap_y : tap_y + row_count, tap_x : tap_x + col_count
                    ].reshape(-1)
                )
    return jnp.stack(layers)


def act_backward(pre_act, shifted, weight_b):
    gate_value = jax.nn.sigmoid(pre_act)
    act_value = pre_act * gate_value
    slope = gate_value * (1.0 + pre_act * (1.0 - gate_value))
    grad_raw = jnp.dot(
        weight_b.astype(jnp.float32), shifted, precision=lax.Precision.HIGHEST
    ).reshape(pre_act.shape)
    return (act_value, slope * grad_raw)


def transposed_backward(extended, weight_a, act_in):
    chan_in, coarse_z, coarse_y, coarse_x = act_in.shape
    chan_out = extended.shape[0]
    split = extended.reshape(chan_out, coarse_z + 1, 2, coarse_y + 1, 2, coarse_x + 1, 2)
    split = split.transpose(0, 2, 4, 6, 1, 3, 5)
    blocks = []
    for tap_z in range(4):
        for tap_y in range(4):
            for tap_x in range(4):
                blocks.append(
                    split[
                        :,
                        tap_z % 2,
                        tap_y % 2,
                        tap_x % 2,
                        tap_z // 2 : tap_z // 2 + coarse_z,
                        tap_y // 2 : tap_y // 2 + coarse_y,
                        tap_x // 2 : tap_x // 2 + coarse_x,
                    ].reshape(chan_out, -1)
                )
    stacked = jnp.concatenate(blocks, axis=0)
    grad_in = jnp.dot(weight_a, stacked, preferred_element_type=jnp.float32)
    grad_wa = lax.dot_general(
        act_in.reshape(chan_in, -1),
        stacked,
        (((1,), (1,)), ((), ())),
        preferred_element_type=jnp.float32,
    )
    return (grad_in.reshape(act_in.shape).astype(jnp.bfloat16), grad_wa)


def body(activations, grad_image, pose_bin, shift, weight_a, bias_a, weight_b):
    act_in = activations[0]
    chan_in, coarse_z, coarse_y, coarse_x = act_in.shape
    chan_out = bias_a.shape[0]
    depth_dev, row_count, col_count = (2 * coarse_z, 2 * coarse_y, 2 * coarse_x)
    slab_count = lax.axis_size("slab")
    total_depth = depth_dev * slab_count
    image_rows = grad_image.shape[1] * slab_count
    first_plane = lax.axis_index("slab") * depth_dev
    angle_bin = pose_bin[0]
    offset = shift[0]
    margin = 1
    planes = depth_dev + 2 * margin
    rows_block = lax.all_gather(grad_image, "slab", axis=1, tiled=True)
    weights = interp_weights(
        angle_bin,
        offset,
        first_plane - margin,
        planes,
        row_count,
        total_depth,
        rows_block.shape[1],
        image_rows,
        NBINS,
    )
    grad_volume = jnp.dot(
        weights, rows_block[0].astype(jnp.float32), precision=lax.Precision.HIGHEST
    )
    plane_ids = first_plane - margin + jnp.arange(planes, dtype=jnp.int32)
    inside = (plane_ids >= 0) & (plane_ids < total_depth)
    grad_volume = jnp.where(
        inside[:, None, None], grad_volume.reshape(planes, row_count, col_count), 0.0
    )
    padded_grad = jnp.pad(grad_volume, ((0, 0), (1, 1), (1, 1)))
    shifted = shifted_stack(padded_grad, planes - 2, row_count, col_count)
    coarse = extended_2(act_in, (("slab", 1),), 1)
    padded_in = jnp.pad(coarse, ((0, 0), (0, 0), (1, 1), (1, 1)))
    pre_act = transposed_forward(padded_in, weight_a, bias_a, (0, 0), coarse_z)
    act_value, grad_raw = act_backward(pre_act, shifted, weight_b)
    extended = extended_2(grad_raw.astype(jnp.bfloat16), (("slab", 1),), 1)
    extended = jnp.pad(extended, ((0, 0), (0, 0), (1, 1), (1, 1)))
    grad_in, grad_wa = transposed_backward(extended, weight_a, act_in)
    local_grad = extended[:, 1:-1, 1:-1, 1:-1]
    grad_ba = jnp.sum(local_grad.astype(jnp.float32), axis=(1, 2, 3))
    grad_wb = jnp.dot(act_value.reshape(chan_out, -1), shifted.T, precision=lax.Precision.HIGHEST)
    grad_bb = jnp.sum(grad_volume[margin : margin + depth_dev]).reshape(1)
    sums = lax.psum((grad_wa, grad_ba, grad_wb, grad_bb), ("batch", "slab"))
    scale = 1.0 / math.sqrt(
        lax.axis_size("batch") * activations.shape[0] * total_depth * row_count * col_count
    )
    return (grad_in[None], sums[0] * scale, sums[1] * scale, sums[2] * scale, sums[3] * scale)


def solution(mesh):
    return jax.shard_map(
        body,
        mesh=mesh,
        in_specs=(
            P("batch", None, "slab", None, None),
            P("batch", "slab", None),
            P("batch"),
            P("batch"),
            P(),
            P(),
            P(),
        ),
        out_specs=(P("batch", None, "slab", None, None), P(), P(), P(), P()),
        check_vma=False,
    )
```

profile of v0, /device:TPU:0, one launch (start us, length us, event | category | flops | bytes accessed | tf_op | source)
XLA Modules:
  0.0 586.1 jit_solution(14745222808796679083)
XLA Ops:
  8.5 3.1 collective-permute-start
  24.2 15.9 %all_gather.3 = bf16[1,256,256]{2,1,0:T(8,128)(2,1)S(1)} all-gather(bf16[1,32,256]{2,1,0:T(8,128)(2,1)} %param.8), channel_id=1, replica_groups=mesh['batch'=4,'slab'=8] {'slab'}, dimensions={1}, use_global_device_ids=true | all-gather | bytes 147456 | tf_op jit(solution)/shard_map/all_gather | solution.py:152
  43.5 5.5 stack.57
  48.9 2.7 fusion.290
  54.3 13.8 %select_maximum_fusion = bf16[64,3,18,130]{3,2,0,1:T(8,128)(2,1)S(1)} fusion(bf16[64,1,16,128]{3,2,0,1:T(8,128)(2,1)S(1)} %collective-permute-done.1, bf16[64,1,16,128]{3,2,0,1:T(8,128)(2,1)S(1)} %bitcast.869, bf16[64,1,16,128]{3,2,0,1:T(8,128)(2,1)S(1)} %collective-permute-done), kind=kLoop, calls=%fused_computation.7 | loop fusion | flops 8536320 | bytes 1684992 | tf_op jit(solution)/shard_map/concatenate | solution.py:23
  89.5 3.1 copy.180
  92.6 3.7 copy.182
  97.8 3.1 copy.175
  100.9 3.7 copy.181
  104.6 3.3 pad_maximum_fusion
  110.2 2.3 collective-permute-start.2
  113.8 2.3 fusion.55
  116.1 43.1 %all-reduce.3 = (f32[32]{0:T(128)S(1)}, f32[32,27]{1,0:T(8,128)S(1)}, f32[1]{0:T(128)}) all-reduce(f32[32]{0:T(128)S(1)} %convert_reduce_fusion, f32[32,27]{1,0:T(8,128)S(1)} %fusion.55, f32[1]{0:T(128)} %bitcast.75), channel_id=1, replica_groups=mesh['batch'=4,'slab'=8] {'batch','slab'}, use_global_device_ids=true, to_apply=%region_2.3 | all-reduce | flops 897 | bytes 7176 | tf_op jit(solution)/shard_map/psum | solution.py:185
  163.2 7.0 %copy.249 = bf16[32,4,32,256]{0,1,3,2:T(4,128)(2,1)} copy(bf16[32,4,32,256]{3,2,1,0:T(8,128)(2,1)S(1)} %pad_maximum_fusion.1) | data formatting | bytes 4194304
  170.3 6.4 %pad.14.clone = bf16[32,4,34,258]{0,1,3,2:T(4,128)(2,1)S(1)} pad(bf16[32,4,32,256]{0,1,3,2:T(4,128)(2,1)} %copy.249, bf16[]{:T(256)} %constant.16.clone.1), padding=0_0x0_0x1_1x1_1 | pad | bytes 4342786 | tf_op jit(solution)/shard_map/jit(_pad)/pad | solution.py:179
  176.7 8.5 %fusion.286 = (bf16[32,1,1,1,1,16,128]{0,1,4,3,6,2,5:T(2,128)(2,1)}, bf16[32,1,1,1,1,16,128]{0,1,4,3,6,2,5:T(2,128)(2,1)}, bf16[32,1,1,1,1,16,128]{0,1,4,3,6,2,5...) fusion(bf16[32,2,2,2,2,17,129]{0,1,4,3,6,2,5:T(2,128)(2,1)S(1)}, ...), kind=kLoop, calls=%fused_computation.461 | loop fusion | bytes 1835008 | tf_op jit(solution)/shard_map/slice | solution.py:118
  185.2 20.9 %fusion.285 = (bf16[32,1,1,1,1,16,128]{0,1,4,3,6,2,5:T(2,128)(2,1)}, bf16[32,1,1,1,1,16,128]{0,1,4,3,6,2,5:T(2,128)(2,1)}, bf16[32,1,1,1,1,16,128]{0,1,4,3,6,2,5...) fusion(bf16[32,2,2,2,2,17,129]{0,1,4,3,6,2,5:T(2,128)(2,1)S(1)}, ...), kind=kLoop, calls=%fused_computation.460 | loop fusion | bytes 4980736 | tf_op jit(solution)/shard_map/slice | solution.py:118
  206.0 23.6 %fusion.283 = (bf16[32,1,1,1,1,16,128]{0,1,4,3,6,2,5:T(2,128)(2,1)}, bf16[32,1,1,1,1,16,128]{0,1,4,3,6,2,5:T(2,128)(2,1)}, bf16[32,1,1,1,1,16,128]{0,1,4,3,6,2,5...) fusion(bf16[32,2,2,2,2,17,129]{0,1,4,3,6,2,5:T(2,128)(2,1)S(1)}, ...), kind=kLoop, calls=%fused_computation.458 | loop fusion | bytes 4980736 | tf_op jit(solution)/shard_map/slice | solution.py:118
  229.6 21.6 %fusion.284 = (bf16[32,1,1,1,1,16,128]{0,1,4,3,6,2,5:T(2,128)(2,1)}, bf16[32,1,1,1,1,16,128]{0,1,4,3,6,2,5:T(2,128)(2,1)}, bf16[32,1,1,1,1,16,128]{0,1,4,3,6,2,5...) fusion(bf16[32,2,2,2,2,17,129]{0,1,4,3,6,2,5:T(2,128)(2,1)S(1)}, ...), kind=kLoop, calls=%fused_computation.459 | loop fusion | bytes 4980736 | tf_op jit(solution)/shard_map/slice | solution.py:118
  251.2 2.1 copy.190
  253.2 2.1 copy.189
  255.3 2.1 copy.188
  257.4 2.1 copy.187
  262.8 2.1 copy.209
  264.9 2.1 copy.208
  269.0 2.1 copy.206
  271.1 2.1 copy.205
  273.2 2.1 copy.204
  275.3 2.1 copy.203
  277.4 2.1 copy.202
  284.9 2.2 copy.197
  287.0 2.1 copy.196
  289.1 2.1 copy.195
  291.2 2.1 copy.194
  295.4 2.1 copy.192
  297.5 2.1 copy.191
  301.1 2.1 copy.246
  303.1 2.1 copy.245
  305.2 2.1 copy.244
  307.3 2.1 copy.243
  312.6 2.2 copy.239
  314.8 2.1 copy.238
  316.9 2.1 copy.237
  318.9 2.1 copy.236
  321.0 2.1 copy.235
  323.1 2.1 copy.234
  325.2 2.1 copy.233
  327.3 2.1 copy.232
  331.5 2.1 copy.230
  333.6 2.1 copy.229
  335.6 2.1 copy.228
  340.9 2.2 copy.224
  345.1 2.1 copy.222
  349.3 2.1 copy.220
  351.4 2.1 copy.219
  353.5 2.1 copy.218
  355.5 2.1 copy.217
  357.6 2.1 copy.216
  359.7 2.1 copy.215
  361.8 2.1 copy.214
  363.9 2.1 copy.213
  441.4 6.8 %convolution_bitcast_fusion = f32[64,2048]{1,0:T(8,128)} fusion(bf16[2048,2048]{1,0:T(8,128)(2,1)} %constant_dynamic-update-slice_fusion, bf16[8,8,16,128]{3,2,1,0:T(8,128)(2,1)S(1)} %bitcast.870), kind=kOutput, calls=%fused_computation.12 | convolution fusion | flops 536870912 | bytes 9175040 | tf_op jit(solution)/shard_map/dot_general | solution.py:130
  448.2 5.0 fusion.66
  454.0 122.1 %all-reduce.6.cloned.1.call-done = f32[64,2048]{1,0:T(8,128)} async-done(((f32[64,2048]{1,0:T(8,128)}), f32[64,2048]{1,0:T(8,128)}) %all-reduce.6.cloned.1.call-update) | async-done | bytes 524304 | tf_op jit(solution)/shard_map/psum | solution.py:185
  (326 shorter events, 152.0 us)
Async XLA Ops:
  7.2 41.8 %copy-start = (bf16[32,27]{1,0:T(8,128)(2,1)S(1)}, bf16[32,27]{1,0:T(8,128)(2,1)}, u32[]{:S(2)}) copy-start(bf16[32,27]{1,0:T(8,128)(2,1)} %param.13) | copy-start | bytes 5188
  7.2 568.9 %all-reduce.6.cloned.1.call-start = ((), (), s32[]{:S(2)}) async-start(), calls=%async_computation | async-start | bytes 1048576 | tf_op jit(solution)/shard_map/psum | solution.py:185
  7.2 47.0 %collective-permute-start.1 = (bf16[64,1,16,128]{3,2,0,1:T(8,128)(2,1)}, bf16[64,1,16,128]{3,2,0,1:T(8,128)(2,1)S(1)}, u32[]{:S(2)}, u32[]{:S(2)}) collective-permute-start(bf16[64,1,16,128]{3,2,0,1:T(8,128)(2,1)} %bitcast.859), channel_id=1, source_target_pairs={{1,0},{2,1},{3,2},{4,3},{5,4},{6,5},{7,6},{9,8},{10,9},{11,10},{12... | collective-permute-start | bytes 786440 | tf_op jit(solution)/shard_map/ppermute | solution.py:22
  8.5 45.7 %collective-permute-start = (bf16[64,1,16,128]{3,2,0,1:T(8,128)(2,1)}, bf16[64,1,16,128]{3,2,0,1:T(8,128)(2,1)S(1)}, u32[]{:S(2)}, u32[]{:S(2)}) collective-permute-start(bf16[64,1,16,128]{3,2,0,1:T(8,128)(2,1)} %bitcast.860), channel_id=1, source_target_pairs={{0,1},{1,2},{2,3},{3,4},{4,5},{5,6},{6,7},{8,9},{9,10},{10,11},{11... | collective-permute-start | bytes 786440 | tf_op jit(solution)/shard_map/ppermute | solution.py:21
  16.3 35.3 %copy-start.2 = (bf16[1,64,1,16,128]{4,3,2,1,0:T(8,128)(2,1)S(1)}, bf16[1,64,1,16,128]{4,3,2,1,0:T(8,128)(2,1)}, u32[]{:S(2)}) copy-start(bf16[1,64,1,16,128]{4,3,2,1,0:T(8,128)(2,1)} %param.7) | copy-start | bytes 786436
  16.3 35.3 %copy-start.3 = (bf16[64,2048]{1,0:T(8,128)(2,1)S(1)}, bf16[64,2048]{1,0:T(8,128)(2,1)}, u32[]{:S(2)}) copy-start(bf16[64,2048]{1,0:T(8,128)(2,1)} %param.11) | copy-start | bytes 786436
  72.8 8.0 %copy-start.22 = (f32[32,2048]{1,0:T(8,128)S(1)}, f32[32,2048]{1,0:T(8,128)}, u32[]{:S(2)}) copy-start(f32[32,2048]{1,0:T(8,128)} %fusion.140) | copy-start | bytes 786436
  74.9 6.9 %copy-start.21 = (f32[32,2048]{1,0:T(8,128)S(1)}, f32[32,2048]{1,0:T(8,128)}, u32[]{:S(2)}) copy-start(f32[32,2048]{1,0:T(8,128)} %fusion.134) | copy-start | bytes 786436
  76.8 5.9 %copy-start.20 = (f32[32,2048]{1,0:T(8,128)S(1)}, f32[32,2048]{1,0:T(8,128)}, u32[]{:S(2)}) copy-start(f32[32,2048]{1,0:T(8,128)} %fusion.136) | copy-start | bytes 786436
  78.6 5.0 copy-start.19
  79.8 5.6 copy-start.18
  96.4 8.2 %copy-start.54 = (f32[32]{0:T(128)S(1)}, f32[32]{0:T(128)}, u32[]{:S(2)}) copy-start(f32[32]{0:T(128)} %param.12) | copy-start | bytes 388
  104.6 9.2 %copy-start.5 = (f32[27,16384]{1,0:T(8,128)S(1)}, f32[27,16384]{1,0:T(8,128)}, u32[]{:S(2)}) copy-start(f32[27,16384]{1,0:T(8,128)} %stack.57) | copy-start | bytes 5308420
  110.2 50.8 %collective-permute-start.2 = (bf16[32,1,32,256]{3,2,1,0:T(8,128)(2,1)S(1)}, bf16[32,1,32,256]{3,2,1,0:T(8,128)(2,1)S(1)}, u32[]{:S(2)}, u32[]{:S(2)}) collective-permute-start(bf16[32,1,32,256]{3,2,1,0:T(8,128)(2,1)S(1)} %get-tuple-element.118), channel_id=1, source_target_pairs={{0,1},{1,2},{2,3},{3,4},{4,5},{5,6},{6,7},{8,9},{9,10},{10,11},{11... | collective-permute-start | bytes 1572872 | tf_op jit(solution)/shard_map/ppermute | solution.py:21
  112.5 49.3 %collective-permute-start.3 = (bf16[32,1,32,256]{3,2,1,0:T(8,128)(2,1)S(1)}, bf16[32,1,32,256]{3,2,1,0:T(8,128)(2,1)}, u32[]{:S(2)}, u32[]{:S(2)}) collective-permute-start(bf16[32,1,32,256]{3,2,1,0:T(8,128)(2,1)S(1)} %get-tuple-element.119), channel_id=1, source_target_pairs={{1,0},{2,1},{3,2},{4,3},{5,4},{6,5},{7,6},{9,8},{10,9},{11,10},{12... | collective-permute-start | bytes 1572872 | tf_op jit(solution)/shard_map/ppermute | solution.py:22
  161.0 0.8 copy-start.53
  260.6 20.9 %copy-start.17 = (bf16[32,1,1,1,1,16,128]{0,1,4,3,6,2,5:T(2,128)(2,1)S(1)}, bf16[32,1,1,1,1,16,128]{0,1,4,3,6,2,5:T(2,128)(2,1)}, u32[]{:S(2)}) copy-start(bf16[32,1,1,1,1,16,128]{0,1,4,3,6,2,5:T(2,128)(2,1)} %get-tuple-element.75) | copy-start | bytes 393220
  261.6 21.0 %copy-start.16 = (bf16[32,1,1,1,1,16,128]{0,1,4,3,6,2,5:T(2,128)(2,1)S(1)}, bf16[32,1,1,1,1,16,128]{0,1,4,3,6,2,5:T(2,128)(2,1)}, u32[]{:S(2)}) copy-start(bf16[32,1,1,1,1,16,128]{0,1,4,3,6,2,5:T(2,128)(2,1)} %get-tuple-element.76) | copy-start | bytes 393220
  262.1 21.7 %copy-start.15 = (bf16[32,1,1,1,1,16,128]{0,1,4,3,6,2,5:T(2,128)(2,1)S(1)}, bf16[32,1,1,1,1,16,128]{0,1,4,3,6,2,5:T(2,128)(2,1)}, u32[]{:S(2)}) copy-start(bf16[32,1,1,1,1,16,128]{0,1,4,3,6,2,5:T(2,128)(2,1)} %get-tuple-element.77) | copy-start | bytes 393220
  282.6 26.8 %copy-start.14 = (bf16[32,1,1,1,1,16,128]{0,1,4,3,6,2,5:T(2,128)(2,1)S(1)}, bf16[32,1,1,1,1,16,128]{0,1,4,3,6,2,5:T(2,128)(2,1)}, u32[]{:S(2)}) copy-start(bf16[32,1,1,1,1,16,128]{0,1,4,3,6,2,5:T(2,128)(2,1)} %get-tuple-element.33) | copy-start | bytes 393220
  283.8 26.7 %copy-start.13 = (bf16[32,1,1,1,1,16,128]{0,1,4,3,6,2,5:T(2,128)(2,1)S(1)}, bf16[32,1,1,1,1,16,128]{0,1,4,3,6,2,5:T(2,128)(2,1)}, u32[]{:S(2)}) copy-start(bf16[32,1,1,1,1,16,128]{0,1,4,3,6,2,5:T(2,128)(2,1)} %get-tuple-element.34) | copy-start | bytes 393220
  284.9 26.7 %copy-start.12 = (bf16[32,1,1,1,1,16,128]{0,1,4,3,6,2,5:T(2,128)(2,1)S(1)}, bf16[32,1,1,1,1,16,128]{0,1,4,3,6,2,5:T(2,128)(2,1)}, u32[]{:S(2)}) copy-start(bf16[32,1,1,1,1,16,128]{0,1,4,3,6,2,5:T(2,128)(2,1)} %get-tuple-element.35) | copy-start | bytes 393220
  310.4 27.3 %copy-start.11 = (bf16[32,1,1,1,1,16,128]{0,1,4,3,6,2,5:T(2,128)(2,1)S(1)}, bf16[32,1,1,1,1,16,128]{0,1,4,3,6,2,5:T(2,128)(2,1)}, u32[]{:S(2)}) copy-start(bf16[32,1,1,1,1,16,128]{0,1,4,3,6,2,5:T(2,128)(2,1)} %get-tuple-element.48) | copy-start | bytes 393220
  311.5 27.3 %copy-start.10 = (bf16[32,1,1,1,1,16,128]{0,1,4,3,6,2,5:T(2,128)(2,1)S(1)}, bf16[32,1,1,1,1,16,128]{0,1,4,3,6,2,5:T(2,128)(2,1)}, u32[]{:S(2)}) copy-start(bf16[32,1,1,1,1,16,128]{0,1,4,3,6,2,5:T(2,128)(2,1)} %get-tuple-element.49) | copy-start | bytes 393220
  312.6 27.3 %copy-start.9 = (bf16[32,1,1,1,1,16,128]{0,1,4,3,6,2,5:T(2,128)(2,1)S(1)}, bf16[32,1,1,1,1,16,128]{0,1,4,3,6,2,5:T(2,128)(2,1)}, u32[]{:S(2)}) copy-start(bf16[32,1,1,1,1,16,128]{0,1,4,3,6,2,5:T(2,128)(2,1)} %get-tuple-element.50) | copy-start | bytes 393220
  338.8 27.2 %copy-start.8 = (bf16[32,1,1,1,1,16,128]{0,1,4,3,6,2,5:T(2,128)(2,1)S(1)}, bf16[32,1,1,1,1,16,128]{0,1,4,3,6,2,5:T(2,128)(2,1)}, u32[]{:S(2)}) copy-start(bf16[32,1,1,1,1,16,128]{0,1,4,3,6,2,5:T(2,128)(2,1)} %get-tuple-element.63) | copy-start | bytes 393220
  339.8 27.2 %copy-start.7 = (bf16[32,1,1,1,1,16,128]{0,1,4,3,6,2,5:T(2,128)(2,1)S(1)}, bf16[32,1,1,1,1,16,128]{0,1,4,3,6,2,5:T(2,128)(2,1)}, u32[]{:S(2)}) copy-start(bf16[32,1,1,1,1,16,128]{0,1,4,3,6,2,5:T(2,128)(2,1)} %get-tuple-element.64) | copy-start | bytes 393220
  340.9 27.3 %copy-start.6 = (bf16[32,1,1,1,1,16,128]{0,1,4,3,6,2,5:T(2,128)(2,1)S(1)}, bf16[32,1,1,1,1,16,128]{0,1,4,3,6,2,5:T(2,128)(2,1)}, u32[]{:S(2)}) copy-start(bf16[32,1,1,1,1,16,128]{0,1,4,3,6,2,5:T(2,128)(2,1)} %get-tuple-element.65) | copy-start | bytes 393220
  367.1 64.8 %copy-start.35 = (bf16[32,1,1,1,1,16,128]{6,5,0,4,3,2,1:T(8,128)(2,1)S(1)}, bf16[32,1,1,1,1,16,128]{6,5,0,4,3,2,1:T(8,128)(2,1)}, u32[]{:S(2)}) copy-start(bf16[32,1,1,1,1,16,128]{6,5,0,4,3,2,1:T(8,128)(2,1)} %copy.234) | copy-start | bytes 393220
  367.1 65.5 %copy-start.34 = (bf16[32,1,1,1,1,16,128]{6,5,0,4,3,2,1:T(8,128)(2,1)S(1)}, bf16[32,1,1,1,1,16,128]{6,5,0,4,3,2,1:T(8,128)(2,1)}, u32[]{:S(2)}) copy-start(bf16[32,1,1,1,1,16,128]{6,5,0,4,3,2,1:T(8,128)(2,1)} %copy.235) | copy-start | bytes 393220
  367.1 66.2 %copy-start.33 = (bf16[32,1,1,1,1,16,128]{6,5,0,4,3,2,1:T(8,128)(2,1)S(1)}, bf16[32,1,1,1,1,16,128]{6,5,0,4,3,2,1:T(8,128)(2,1)}, u32[]{:S(2)}) copy-start(bf16[32,1,1,1,1,16,128]{6,5,0,4,3,2,1:T(8,128)(2,1)} %copy.236) | copy-start | bytes 393220
  367.1 66.8 %copy-start.32 = (bf16[32,1,1,1,1,16,128]{6,5,0,4,3,2,1:T(8,128)(2,1)S(1)}, bf16[32,1,1,1,1,16,128]{6,5,0,4,3,2,1:T(8,128)(2,1)}, u32[]{:S(2)}) copy-start(bf16[32,1,1,1,1,16,128]{6,5,0,4,3,2,1:T(8,128)(2,1)} %copy.237) | copy-start | bytes 393220
  367.1 67.5 %copy-start.31 = (bf16[32,1,1,1,1,16,128]{6,5,0,4,3,2,1:T(8,128)(2,1)S(1)}, bf16[32,1,1,1,1,16,128]{6,5,0,4,3,2,1:T(8,128)(2,1)}, u32[]{:S(2)}) copy-start(bf16[32,1,1,1,1,16,128]{6,5,0,4,3,2,1:T(8,128)(2,1)} %copy.238) | copy-start | bytes 393220
  367.1 68.2 %copy-start.30 = (bf16[32,1,1,1,1,16,128]{6,5,0,4,3,2,1:T(8,128)(2,1)S(1)}, bf16[32,1,1,1,1,16,128]{6,5,0,4,3,2,1:T(8,128)(2,1)}, u32[]{:S(2)}) copy-start(bf16[32,1,1,1,1,16,128]{6,5,0,4,3,2,1:T(8,128)(2,1)} %copy.239) | copy-start | bytes 393220
  367.1 68.8 %copy-start.29 = (bf16[32,1,1,1,1,16,128]{6,5,0,4,3,2,1:T(8,128)(2,1)S(1)}, bf16[32,1,1,1,1,16,128]{6,5,0,4,3,2,1:T(8,128)(2,1)}, u32[]{:S(2)}) copy-start(bf16[32,1,1,1,1,16,128]{6,5,0,4,3,2,1:T(8,128)(2,1)} %copy.240) | copy-start | bytes 393220
  367.1 69.5 %copy-start.28 = (bf16[32,1,1,1,1,16,128]{6,5,0,4,3,2,1:T(8,128)(2,1)S(1)}, bf16[32,1,1,1,1,16,128]{6,5,0,4,3,2,1:T(8,128)(2,1)}, u32[]{:S(2)}) copy-start(bf16[32,1,1,1,1,16,128]{6,5,0,4,3,2,1:T(8,128)(2,1)} %copy.241) | copy-start | bytes 393220
  368.2 61.6 %copy-start.38 = (bf16[32,1,1,1,1,16,128]{6,5,0,4,3,2,1:T(8,128)(2,1)S(1)}, bf16[32,1,1,1,1,16,128]{6,5,0,4,3,2,1:T(8,128)(2,1)}, u32[]{:S(2)}) copy-start(bf16[32,1,1,1,1,16,128]{6,5,0,4,3,2,1:T(8,128)(2,1)} %copy.231) | copy-start | bytes 393220
  368.2 62.3 %copy-start.37 = (bf16[32,1,1,1,1,16,128]{6,5,0,4,3,2,1:T(8,128)(2,1)S(1)}, bf16[32,1,1,1,1,16,128]{6,5,0,4,3,2,1:T(8,128)(2,1)}, u32[]{:S(2)}) copy-start(bf16[32,1,1,1,1,16,128]{6,5,0,4,3,2,1:T(8,128)(2,1)} %copy.232) | copy-start | bytes 393220
  368.2 63.0 %copy-start.36 = (bf16[32,1,1,1,1,16,128]{6,5,0,4,3,2,1:T(8,128)(2,1)S(1)}, bf16[32,1,1,1,1,16,128]{6,5,0,4,3,2,1:T(8,128)(2,1)}, u32[]{:S(2)}) copy-start(bf16[32,1,1,1,1,16,128]{6,5,0,4,3,2,1:T(8,128)(2,1)} %copy.233) | copy-start | bytes 393220
  368.2 69.1 %copy-start.27 = (bf16[32,1,1,1,1,16,128]{6,5,0,4,3,2,1:T(8,128)(2,1)S(1)}, bf16[32,1,1,1,1,16,128]{6,5,0,4,3,2,1:T(8,128)(2,1)}, u32[]{:S(2)}) copy-start(bf16[32,1,1,1,1,16,128]{6,5,0,4,3,2,1:T(8,128)(2,1)} %copy.242) | copy-start | bytes 393220
  368.2 69.8 %copy-start.26 = (bf16[32,1,1,1,1,16,128]{6,5,0,4,3,2,1:T(8,128)(2,1)S(1)}, bf16[32,1,1,1,1,16,128]{6,5,0,4,3,2,1:T(8,128)(2,1)}, u32[]{:S(2)}) copy-start(bf16[32,1,1,1,1,16,128]{6,5,0,4,3,2,1:T(8,128)(2,1)} %copy.243) | copy-start | bytes 393220
  368.2 70.4 %copy-start.25 = (bf16[32,1,1,1,1,16,128]{6,5,0,4,3,2,1:T(8,128)(2,1)S(1)}, bf16[32,1,1,1,1,16,128]{6,5,0,4,3,2,1:T(8,128)(2,1)}, u32[]{:S(2)}) copy-start(bf16[32,1,1,1,1,16,128]{6,5,0,4,3,2,1:T(8,128)(2,1)} %copy.244) | copy-start | bytes 393220
  368.2 71.1 %copy-start.24 = (bf16[32,1,1,1,1,16,128]{6,5,0,4,3,2,1:T(8,128)(2,1)S(1)}, bf16[32,1,1,1,1,16,128]{6,5,0,4,3,2,1:T(8,128)(2,1)}, u32[]{:S(2)}) copy-start(bf16[32,1,1,1,1,16,128]{6,5,0,4,3,2,1:T(8,128)(2,1)} %copy.245) | copy-start | bytes 393220
  368.2 71.8 %copy-start.23 = (bf16[32,1,1,1,1,16,128]{6,5,0,4,3,2,1:T(8,128)(2,1)S(1)}, bf16[32,1,1,1,1,16,128]{6,5,0,4,3,2,1:T(8,128)(2,1)}, u32[]{:S(2)}) copy-start(bf16[32,1,1,1,1,16,128]{6,5,0,4,3,2,1:T(8,128)(2,1)} %copy.246) | copy-start | bytes 393220
  369.5 50.8 %copy-start.52 = (bf16[32,1,1,1,1,16,128]{6,5,0,4,3,2,1:T(8,128)(2,1)S(1)}, bf16[32,1,1,1,1,16,128]{6,5,0,4,3,2,1:T(8,128)(2,1)}, u32[]{:S(2)}) copy-start(bf16[32,1,1,1,1,16,128]{6,5,0,4,3,2,1:T(8,128)(2,1)} %copy.217) | copy-start | bytes 393220
  369.5 51.5 %copy-start.51 = (bf16[32,1,1,1,1,16,128]{6,5,0,4,3,2,1:T(8,128)(2,1)S(1)}, bf16[32,1,1,1,1,16,128]{6,5,0,4,3,2,1:T(8,128)(2,1)}, u32[]{:S(2)}) copy-start(bf16[32,1,1,1,1,16,128]{6,5,0,4,3,2,1:T(8,128)(2,1)} %copy.218) | copy-start | bytes 393220
  369.5 52.2 %copy-start.50 = (bf16[32,1,1,1,1,16,128]{6,5,0,4,3,2,1:T(8,128)(2,1)S(1)}, bf16[32,1,1,1,1,16,128]{6,5,0,4,3,2,1:T(8,128)(2,1)}, u32[]{:S(2)}) copy-start(bf16[32,1,1,1,1,16,128]{6,5,0,4,3,2,1:T(8,128)(2,1)} %copy.219) | copy-start | bytes 393220
  369.5 52.8 %copy-start.49 = (bf16[32,1,1,1,1,16,128]{6,5,0,4,3,2,1:T(8,128)(2,1)S(1)}, bf16[32,1,1,1,1,16,128]{6,5,0,4,3,2,1:T(8,128)(2,1)}, u32[]{:S(2)}) copy-start(bf16[32,1,1,1,1,16,128]{6,5,0,4,3,2,1:T(8,128)(2,1)} %copy.220) | copy-start | bytes 393220
  369.5 53.5 %copy-start.48 = (bf16[32,1,1,1,1,16,128]{6,5,0,4,3,2,1:T(8,128)(2,1)S(1)}, bf16[32,1,1,1,1,16,128]{6,5,0,4,3,2,1:T(8,128)(2,1)}, u32[]{:S(2)}) copy-start(bf16[32,1,1,1,1,16,128]{6,5,0,4,3,2,1:T(8,128)(2,1)} %copy.221) | copy-start | bytes 393220
  369.6 54.2 %copy-start.47 = (bf16[32,1,1,1,1,16,128]{6,5,0,4,3,2,1:T(8,128)(2,1)S(1)}, bf16[32,1,1,1,1,16,128]{6,5,0,4,3,2,1:T(8,128)(2,1)}, u32[]{:S(2)}) copy-start(bf16[32,1,1,1,1,16,128]{6,5,0,4,3,2,1:T(8,128)(2,1)} %copy.222) | copy-start | bytes 393220
  369.6 54.9 %copy-start.46 = (bf16[32,1,1,1,1,16,128]{6,5,0,4,3,2,1:T(8,128)(2,1)S(1)}, bf16[32,1,1,1,1,16,128]{6,5,0,4,3,2,1:T(8,128)(2,1)}, u32[]{:S(2)}) copy-start(bf16[32,1,1,1,1,16,128]{6,5,0,4,3,2,1:T(8,128)(2,1)} %copy.223) | copy-start | bytes 393220
  369.6 55.5 %copy-start.45 = (bf16[32,1,1,1,1,16,128]{6,5,0,4,3,2,1:T(8,128)(2,1)S(1)}, bf16[32,1,1,1,1,16,128]{6,5,0,4,3,2,1:T(8,128)(2,1)}, u32[]{:S(2)}) copy-start(bf16[32,1,1,1,1,16,128]{6,5,0,4,3,2,1:T(8,128)(2,1)} %copy.224) | copy-start | bytes 393220
  369.6 56.2 %copy-start.44 = (bf16[32,1,1,1,1,16,128]{6,5,0,4,3,2,1:T(8,128)(2,1)S(1)}, bf16[32,1,1,1,1,16,128]{6,5,0,4,3,2,1:T(8,128)(2,1)}, u32[]{:S(2)}) copy-start(bf16[32,1,1,1,1,16,128]{6,5,0,4,3,2,1:T(8,128)(2,1)} %copy.225) | copy-start | bytes 393220
  369.6 56.9 %copy-start.43 = (bf16[32,1,1,1,1,16,128]{6,5,0,4,3,2,1:T(8,128)(2,1)S(1)}, bf16[32,1,1,1,1,16,128]{6,5,0,4,3,2,1:T(8,128)(2,1)}, u32[]{:S(2)}) copy-start(bf16[32,1,1,1,1,16,128]{6,5,0,4,3,2,1:T(8,128)(2,1)} %copy.226) | copy-start | bytes 393220
  369.6 57.5 %copy-start.42 = (bf16[32,1,1,1,1,16,128]{6,5,0,4,3,2,1:T(8,128)(2,1)S(1)}, bf16[32,1,1,1,1,16,128]{6,5,0,4,3,2,1:T(8,128)(2,1)}, u32[]{:S(2)}) copy-start(bf16[32,1,1,1,1,16,128]{6,5,0,4,3,2,1:T(8,128)(2,1)} %copy.227) | copy-start | bytes 393220
  369.6 58.2 %copy-start.41 = (bf16[32,1,1,1,1,16,128]{6,5,0,4,3,2,1:T(8,128)(2,1)S(1)}, bf16[32,1,1,1,1,16,128]{6,5,0,4,3,2,1:T(8,128)(2,1)}, u32[]{:S(2)}) copy-start(bf16[32,1,1,1,1,16,128]{6,5,0,4,3,2,1:T(8,128)(2,1)} %copy.228) | copy-start | bytes 393220
  369.6 58.9 %copy-start.40 = (bf16[32,1,1,1,1,16,128]{6,5,0,4,3,2,1:T(8,128)(2,1)S(1)}, bf16[32,1,1,1,1,16,128]{6,5,0,4,3,2,1:T(8,128)(2,1)}, u32[]{:S(2)}) copy-start(bf16[32,1,1,1,1,16,128]{6,5,0,4,3,2,1:T(8,128)(2,1)} %copy.229) | copy-start | bytes 393220
  369.6 59.5 %copy-start.39 = (bf16[32,1,1,1,1,16,128]{6,5,0,4,3,2,1:T(8,128)(2,1)S(1)}, bf16[32,1,1,1,1,16,128]{6,5,0,4,3,2,1:T(8,128)(2,1)}, u32[]{:S(2)}) copy-start(bf16[32,1,1,1,1,16,128]{6,5,0,4,3,2,1:T(8,128)(2,1)} %copy.230) | copy-start | bytes 393220
  430.5 17.7 %copy-start.4 = (bf16[64,2048]{1,0:T(8,128)(2,1)S(1)}, bf16[64,2048]{1,0:T(8,128)(2,1)}, u32[]{:S(2)}) copy-start(bf16[64,2048]{1,0:T(8,128)(2,1)} %param.11) | copy-start | bytes 786436
  448.2 129.7 %copy-start.1 = (bf16[32,27]{1,0:T(8,128)(2,1)S(1)}, bf16[32,27]{1,0:T(8,128)(2,1)}, u32[]{:S(2)}) copy-start(bf16[32,27]{1,0:T(8,128)(2,1)} %param.13) | copy-start | bytes 5188
Sparse Core Ops, SparseCore 0:
  448.3 127.6 all-reduce.5
where the time goes:
time: 589 us; the launch traced here: 586 us
  local copies, waits for them, and re-layouts  309 us (52%)
  waiting for transfers between devices  122 us (21%)
  blocking collectives  59 us (10%)
  matrix products  43.9 us (7%)
  other arithmetic  24.9 us (4%)
  between operations  18.9 us (3%)
  starting transfers between devices  7.94 us (1%)
    slice x68, local copies, waits for them, and re-layouts, transposed_backward(): split[:, tap_z % 2, tap_y % 2, tap_x % 2, tap_z // 2:tap_z // 2 + coarse_...  192 us
    psum x1, waiting for transfers between devices, body(): sums = lax.psum((grad_wa, grad_ba, grad_wb, grad_bb), ('batch', 'slab'))  122 us
    unnamed x185, local copies, waits for them, and re-layouts  86.9 us
    psum x1, blocking collectives, body(): sums = lax.psum((grad_wa, grad_ba, grad_wb, grad_bb), ('batch', 'slab'))  43.1 us
    dot_general x64, matrix products, transposed_forward(): jnp.dot(matrix.T, block, preferred_element_type=jnp.float32)  26.8 us
    all_gather x1, blocking collectives, body(): rows_block = lax.all_gather(grad_image, 'slab', axis=1, tiled=True)  15.9 us
    concatenate x2, other arithmetic, extended_2(): array = jnp.concatenate([before, array, after], axis=dim)  15.3 us
  transfers between devices with their start and end apart: 5, of which 1 were waited for; matrix products, arithmetic and copies ran while one was open for 6% of the time, Pallas kernels for 0%

commit v1 on v0

v1 whole, which is shorter than its diff:
```python
import functools
import math

import jax
import jax.numpy as jnp
from jax import lax
from jax.experimental import pallas as pl
from jax.experimental.pallas import tpu as pltpu
from jax.sharding import PartitionSpec as P

NBINS = 32
MESH = pl.DeviceIdType.MESH
F32 = jnp.float32
BF16 = jnp.bfloat16
VMEM_LIMIT = 56 * 1024 * 1024


def nt_dot(a, b):
    return lax.dot_general(a, b, (((1,), (1,)), ((), ())), preferred_element_type=F32)


def mm(a, b):
    return jnp.dot(a, b, preferred_element_type=F32)


def gather_kernel(ns, x_ref, img_ref, halo_ref, all_ref, h_send, h_recv, g_send, g_recv):
    mb = lax.axis_index("batch")
    me = lax.axis_index("slab")
    barrier = pltpu.get_barrier_semaphore()
    for d in range(1, ns):
        pl.semaphore_signal(
            barrier, inc=1, device_id=(mb, lax.rem(me + d, ns)), device_id_type=MESH
        )
    pl.semaphore_wait(barrier, ns - 1)

    def to_right():
        return pltpu.make_async_remote_copy(
            src_ref=x_ref,
            dst_ref=halo_ref.at[0],
            send_sem=h_send.at[0],
            recv_sem=h_recv.at[0],
            device_id=(mb, lax.rem(me + 1, ns)),
            device_id_type=MESH,
        )

    def to_left():
        return pltpu.make_async_remote_copy(
            src_ref=x_ref,
            dst_ref=halo_ref.at[1],
            send_sem=h_send.at[1],
            recv_sem=h_recv.at[1],
            device_id=(mb, lax.rem(me + ns - 1, ns)),
            device_id_type=MESH,
        )

    @pl.when(me < ns - 1)
    def _():
        to_right().start()

    @pl.when(me > 0)
    def _():
        to_left().start()

    copies = []
    for d in range(1, ns):
        copy = pltpu.make_async_remote_copy(
            src_ref=img_ref,
            dst_ref=all_ref.at[me],
            send_sem=g_send.at[d - 1],
            recv_sem=g_recv.at[d - 1],
            device_id=(mb, lax.rem(me + d, ns)),
            device_id_type=MESH,
        )
        copy.start()
        copies.append(copy)
    all_ref[me] = img_ref[...]

    @pl.when(me == 0)
    def _():
        halo_ref[0] = jnp.zeros(halo_ref.shape[1:], halo_ref.dtype)

    @pl.when(me == ns - 1)
    def _():
        halo_ref[1] = jnp.zeros(halo_ref.shape[1:], halo_ref.dtype)

    for copy in copies:
        copy.wait()

    @pl.when(me < ns - 1)
    def _():
        to_right().wait_send()
        to_left().wait_recv()

    @pl.when(me > 0)
    def _():
        to_left().wait_send()
        to_right().wait_recv()


def local_kernel(
    ns,
    trig_ref,
    x_ref,
    halo_ref,
    img_ref,
    wa_ref,
    bias_ref,
    wbt_ref,
    gin_ref,
    gwa_ref,
    small_ref,
    tt_ref,
    g_ref,
    gt_ref,
    ga_ref,
    wf_ref,
    w4_ref,
    wb_ref,
    act_ref,
):
    me = lax.axis_index("slab")
    yc_n, c0, xc_n = x_ref.shape
    c1 = 32
    rows = img_ref.shape[0]
    depth = 2 * ns
    height = 2 * yc_n
    pos = yc_n * xc_n

    def iota(shape, dim):
        return lax.broadcasted_iota(jnp.int32, shape, dim)

    w = wa_ref[...]
    lane = iota((c0, 128), 1)
    for g in range(16):
        block = jnp.concatenate(
            [w[:, kz * 512 + g * 32 : kz * 512 + g * 32 + 32] for kz in range(4)], axis=1
        )
        w4_ref[:, g * 128 : (g + 1) * 128] = block
    zero_block = jnp.zeros((c0, 128), BF16)
    for py in range(2):
        for dyi in range(2):
            dy = py - 1 + dyi
            ky = py - 2 * dy + 1
            for dxi in range(3):
                dx = dxi - 1
                for px in range(2):
                    kx = px - 2 * dx + 1
                    for plane in range(3):
                        if 0 <= kx <= 3:
                            g = ky * 4 + kx
                            base = w4_ref[:, g * 128 : (g + 1) * 128]
                            half = jnp.zeros((c0, 64), BF16)
                            if plane == 0:
                                base = jnp.concatenate([base[:, 64:], half], axis=1)
                            elif plane == 2:
                                base = jnp.concatenate([half, base[:, :64]], axis=1)
                        else:
                            base = zero_block
                        wf_ref[
                            py, dyi, dxi, plane * c0 : (plane + 1) * c0, px * 128 : (px + 1) * 128
                        ] = base

    row = iota((96, 512), 0)
    col = iota((96, 512), 1)
    q = col >> 5
    tz, px_c, py_c = (q & 3, (q >> 2) & 1, (q >> 3) & 1)
    tx_r = (
        (row >= 24).astype(jnp.int32)
        + (row >= 48).astype(jnp.int32)
        + (row >= 72).astype(jnp.int32)
    )
    rem = row - 24 * tx_r
    az = (rem >> 2) - tz
    by = (rem & 3) - py_c
    cx = tx_r - px_c
    ok = (az >= 0) & (az < 3) & (by >= 0) & (by < 3) & (cx >= 0) & (cx < 3)
    index = jnp.where(ok, 9 * az + 3 * by + cx, -1)
    inside = ((tz > 0) | (me > 0)) & ((tz < 3) | (me < ns - 1))
    masked_index = jnp.where(inside, index, -1)
    wb_mat = jnp.zeros((96, 512), F32)
    for t in range(27):
        wb_mat = jnp.where(masked_index == t, wbt_ref[t : t + 1, :], wb_mat)
    wb_mat = wb_mat.astype(BF16)
    wb_ref[0:96, :] = wb_mat
    wb_ref[96:192, :] = wb_mat

    width = img_ref.shape[1]
    col_x = iota((width, 512), 1)
    fine = 2 * (col_x & 127) + (col_x >> 7) - 1
    sel = (iota((width, 512), 0) == fine).astype(F32).astype(BF16)
    ims = mm(img_ref[...], sel).astype(BF16)
    shape3 = (yc_n, 24, rows)
    j = iota(shape3, 1)
    y = 2 * iota(shape3, 0) + (j & 3) - 1
    z = 2 * me - 2 + (j >> 2)
    center = (
        (y.astype(F32) - 0.5 * (height - 1)) * trig_ref[0]
        + (z.astype(F32) - 0.5 * (depth - 1)) * trig_ref[1]
        + (0.5 * (rows - 1) + trig_ref[2])
    )
    interp = jnp.maximum(1.0 - jnp.abs(iota(shape3, 2).astype(F32) - center), 0.0)
    interp = jnp.where((y >= 0) & (y < height) & (z >= 0) & (z < depth), interp, 0.0)
    interp = interp.reshape(yc_n * 24, rows)
    hi = interp.astype(BF16)
    lo = (interp - hi.astype(F32)).astype(BF16)
    gtf = mm(hi, ims) + mm(lo, ims)
    eye = (iota((128, 128), 0) == iota((128, 128), 1)).astype(F32).astype(BF16)
    own_rows = iota((24, 256), 0)
    own = ((own_rows >> 2) >= 2) & ((own_rows >> 2) < 4) & ((own_rows & 3) > 0) & ((own_rows & 3) < 3)
    gb_total = jnp.zeros((24, 256), F32)
    sh_row = iota((384, 128), 0)
    shift_mat = (
        iota((384, 128), 1) == (sh_row & 127) + (sh_row >> 7) - 1
    ).astype(F32).astype(BF16)
    pad = jnp.zeros((128, 192), BF16)
    for dxi in range(3):
        tt_ref[dxi, 0:128, :] = pad
        tt_ref[dxi, pos + 128 : pos + 256, :] = pad
    for yc in range(yc_n):
        f = gtf[yc * 24 : (yc + 1) * 24]
        gb_total = gb_total + jnp.where(own, f[:, 128:384], 0.0)
        blk = jnp.concatenate([f[:, tx * 128 : (tx + 1) * 128] for tx in range(4)], axis=0)
        bhi = blk.astype(BF16)
        blo = (blk - bhi.astype(F32)).astype(BF16)
        gt = jnp.concatenate([bhi, blo], axis=0)
        gt_ref[yc] = gt
        g_ref[yc * 128 : (yc + 1) * 128, :] = nt_dot(eye, gt).astype(BF16)
        planes = jnp.concatenate([halo_ref[0, yc], x_ref[yc], halo_ref[1, yc]], axis=0)
        r = nt_dot(shift_mat, planes).astype(BF16)
        for dxi in range(3):
            tt_ref[dxi, (yc + 1) * 128 : (yc + 2) * 128, :] = r[dxi * 128 : (dxi + 1) * 128]

    zpad = jnp.zeros((128, 128), BF16)
    for kx in range(4):
        for py in range(2):
            ga_ref[kx, py, 0:128, :] = zpad
            ga_ref[kx, py, pos + 128 : pos + 256, :] = zpad
    step = 512
    xc_id = iota((step, 128), 0) & 127
    bias = bias_ref[...]

    def forward(it, sums):
        start = pl.multiple_of(it * step, step)
        new = []
        for py in range(2):
            pre = None
            for dyi in range(2):
                for dxi in range(3):
                    base = pl.multiple_of(start + (py + dyi) * 128, 128)
                    term = mm(tt_ref[dxi, pl.ds(base, step), :], wf_ref[py, dyi, dxi])
                    pre = term if pre is None else pre + term
            pre = pre + bias
            raw = mm(g_ref[pl.ds(start, step), :], wb_ref[:, py * 256 : (py + 1) * 256])
            gate = 0.5 * jnp.tanh(0.5 * pre) + 0.5
            act = pre * gate
            ga = (gate + act * (1.0 - gate)) * raw
            act_ref[pl.ds(start, step), py * 256 : (py + 1) * 256] = act.astype(BF16)
            new.append(sums[py] + jnp.sum(ga.reshape(step // 8, 8, 256), axis=0))
            dst = pl.ds(pl.multiple_of(start + 128, 128), step)
            g0, g1 = ga[:, :128], ga[:, 128:]
            ga_ref[1, py, dst, :] = g0.astype(BF16)
            ga_ref[2, py, dst, :] = g1.astype(BF16)
            ga_ref[0, py, dst, :] = jnp.where(xc_id == 0, 0.0, pltpu.roll(g1, 1, 0)).astype(BF16)
            ga_ref[3, py, dst, :] = jnp.where(
                xc_id == 127, 0.0, pltpu.roll(g0, step - 1, 0)
            ).astype(BF16)
        return tuple(new)

    zero_sum = jnp.zeros((8, 256), F32)
    sums = lax.fori_loop(0, pos // step, forward, (zero_sum, zero_sum))

    r_mat = jnp.zeros((192, 512), F32)
    for yc in range(yc_n):
        r_mat = r_mat + mm(gt_ref[yc], act_ref[yc * 128 : (yc + 1) * 128, :])
    r_sum = r_mat[0:96] + r_mat[96:192]
    mine = (tz > 0) & (tz < 3)
    own_index = jnp.where(mine, index, -1)
    lines = []
    for t in range(27):
        lines.append(jnp.sum(jnp.where(own_index == t, r_sum, 0.0), axis=0, keepdims=True))
    ba_row = jnp.sum(jnp.concatenate([sums[0], sums[1]], axis=1), axis=0, keepdims=True)
    lane5 = iota((1, 512), 1)
    tz5 = (lane5 >> 5) & 3
    lines.append(jnp.where((tz5 > 0) & (tz5 < 3), ba_row, 0.0))
    bb_total = jnp.sum(jnp.sum(gb_total, axis=0, keepdims=True), axis=1, keepdims=True)
    lines.append(jnp.where(lane5 == 0, bb_total, 0.0))
    lines.append(jnp.zeros((3, 512), F32))
    packed = jnp.concatenate(lines, axis=0)
    fold = packed[:, 0:128] + packed[:, 128:256] + packed[:, 256:384] + packed[:, 384:512]
    fold = fold + pltpu.roll(fold, 64, 1)
    fold = fold + pltpu.roll(fold, 32, 1)
    small_ref[...] = fold

    ky_src = ((1, 0), (0, 1), (1, 1), (0, 2))

    def patch(g, start, count):
        py, off = ky_src[g // 4]
        return ga_ref[g % 4, py, pl.ds(start + off * 128, count), :]

    def backward(it, carry):
        start = pl.multiple_of(it * step, step)
        total = None
        for pair in range(8):
            s = jnp.concatenate([patch(2 * pair, start, step), patch(2 * pair + 1, start, step)], axis=1)
            term = nt_dot(s, w4_ref[:, pair * 256 : (pair + 1) * 256])
            total = term if total is None else total + term
        total = total.astype(BF16)
        small_eye = eye[:c0, :c0]
        flipped = nt_dot(small_eye, total).astype(BF16)
        for k in range(step // 128):
            gin_ref[it * (step // 128) + k] = flipped[:, k * 128 : (k + 1) * 128]
        return carry

    lax.fori_loop(0, pos // step, backward, 0)
    xt = jnp.concatenate([x_ref[yc] for yc in range(yc_n)], axis=1)
    for pair in range(8):
        s = jnp.concatenate([patch(2 * pair, 0, pos), patch(2 * pair + 1, 0, pos)], axis=1)
        res = mm(xt, s).astype(BF16)
        gwa_ref[2 * pair] = res[:, :128]
        gwa_ref[2 * pair + 1] = res[:, 128:]


def reduce_kernel(
    nb, ns, scale, part_ref, small_ref, out_ref, osmall_ref,
    rb, mid, rs, full, srb, smid, srs, sems_b, sems_s, sems_g, sems_h, sems_x, sems_y,
):
    mb = lax.axis_index("batch")
    me = lax.axis_index("slab")
    barrier = pltpu.get_barrier_semaphore()
    for d in range(1, nb):
        pl.semaphore_signal(barrier, inc=1, device_id=(lax.rem(mb + d, nb), me), device_id_type=MESH)
    for d in range(1, ns):
        pl.semaphore_signal(barrier, inc=1, device_id=(mb, lax.rem(me + d, ns)), device_id_type=MESH)
    pl.semaphore_wait(barrier, nb + ns - 2)

    def send(src, dst, sems, d, device):
        copy = pltpu.make_async_remote_copy(
            src_ref=src,
            dst_ref=dst,
            send_sem=sems.at[0, d - 1],
            recv_sem=sems.at[1, d - 1],
            device_id=device,
            device_id_type=MESH,
        )
        copy.start()
        return copy

    first = []
    for d in range(1, nb):
        to = lax.rem(mb + d, nb)
        first.append(send(part_ref.at[to], rb.at[mb], sems_b, d, (to, me)))
        first.append(send(small_ref, srb.at[mb], sems_x, d, (to, me)))
    rb[mb] = part_ref[mb]
    srb[mb] = small_ref[...]
    for copy in first:
        copy.wait()
    acc = rb[0].astype(F32)
    sacc = srb[0]
    for b in range(1, nb):
        acc = acc + rb[b].astype(F32)
        sacc = sacc + srb[b]
    mid[...] = acc.astype(BF16)
    smid[...] = sacc
    second = []
    for d in range(1, ns):
        to = lax.rem(me + d, ns)
        second.append(send(mid.at[to], rs.at[me], sems_s, d, (mb, to)))
        second.append(send(smid, srs.at[me], sems_y, d, (mb, to)))
    rs[me] = mid[me]
    srs[me] = sacc
    for copy in second:
        copy.wait()
    acc = rs[0].astype(F32)
    sacc = srs[0]
    for s in range(1, ns):
        acc = acc + rs[s].astype(F32)
        sacc = sacc + srs[s]
    osmall_ref[...] = sacc * scale
    full[mb, me] = acc.astype(BF16)
    third = []
    for d in range(1, ns):
        to = lax.rem(me + d, ns)
        third.append(send(full.at[mb, me], full.at[mb, me], sems_g, d, (mb, to)))
    for copy in third:
        copy.wait()
    fourth = []
    for d in range(1, nb):
        to = lax.rem(mb + d, nb)
        fourth.append(send(full.at[mb], full.at[mb], sems_h, d, (to, me)))
    for copy in fourth:
        copy.wait()
    c0 = out_ref.shape[0]
    per = ns // 4
    for ky in range(4):
        groups = [
            full[ky, kx * per : (kx + 1) * per].astype(F32).reshape(c0, 128) * scale
            for kx in range(4)
        ]
        for kz in range(4):
            out_ref[:, kz * 512 + ky * 128 : kz * 512 + (ky + 1) * 128] = jnp.concatenate(
                [g[:, kz * 32 : (kz + 1) * 32] for g in groups], axis=1
            )


def body(nb, ns, activations, grad_image, pose_bin, shift, weight_a, bias_a, weight_b):
    vm = pl.BlockSpec(memory_space=pltpu.VMEM)
    _, c0, _, yc_n, xc_n = activations.shape
    c1 = bias_a.shape[0]
    pos = yc_n * xc_n
    x = activations[0, :, 0].transpose(1, 0, 2)
    img = grad_image[0]
    local_rows, width = img.shape
    halo, gathered = pl.pallas_call(
        functools.partial(gather_kernel, ns),
        out_shape=(
            jax.ShapeDtypeStruct((2,) + x.shape, BF16),
            jax.ShapeDtypeStruct((ns, local_rows, width), BF16),
        ),
        in_specs=[vm, vm],
        out_specs=(vm, vm),
        scratch_shapes=[
            pltpu.SemaphoreType.DMA((2,)),
            pltpu.SemaphoreType.DMA((2,)),
            pltpu.SemaphoreType.DMA((ns - 1,)),
            pltpu.SemaphoreType.DMA((ns - 1,)),
        ],
        compiler_params=pltpu.CompilerParams(
            collective_id=0, has_side_effects=True, vmem_limit_bytes=VMEM_LIMIT
        ),
        name="gather",
    )(x, img)
    angle = (pose_bin[0].astype(F32) + 0.5) * (math.pi / NBINS)
    trig = jnp.stack([jnp.cos(angle), jnp.sin(angle), shift[0].astype(F32)])
    bias_t = jnp.tile(bias_a, 8)[None]
    wbt = jnp.tile(weight_b.astype(F32).T, (1, 16))
    gin, gwa, small = pl.pallas_call(
        functools.partial(local_kernel, ns),
        out_shape=(
            jax.ShapeDtypeStruct((yc_n, c0, xc_n), BF16),
            jax.ShapeDtypeStruct((16, c0, 128), BF16),
            jax.ShapeDtypeStruct((32, 128), F32),
        ),
        in_specs=[pl.BlockSpec(memory_space=pltpu.SMEM)] + [vm] * 6,
        out_specs=(vm, vm, vm),
        scratch_shapes=[
            pltpu.VMEM((3, pos + 256, 192), BF16),
            pltpu.VMEM((pos, 192), BF16),
            pltpu.VMEM((yc_n, 192, 128), BF16),
            pltpu.VMEM((4, 2, pos + 256, 128), BF16),
            pltpu.VMEM((2, 2, 3, 192, 256), BF16),
            pltpu.VMEM((c0, 2048), BF16),
            pltpu.VMEM((192, 512), BF16),
            pltpu.VMEM((pos, 512), BF16),
        ],
        compiler_params=pltpu.CompilerParams(vmem_limit_bytes=VMEM_LIMIT),
        name="local",
    )(trig, x, halo, gathered.reshape(ns * local_rows, width), weight_a, bias_t, wbt)
    r = 256 // ns
    total_cells = nb * 2 * ns * 2 * yc_n * 2 * xc_n
    scale = 1.0 / math.sqrt(total_cells)
    grad_wa, osmall = pl.pallas_call(
        functools.partial(reduce_kernel, nb, ns, scale),
        out_shape=(
            jax.ShapeDtypeStruct(weight_a.shape, F32),
            jax.ShapeDtypeStruct((32, 128), F32),
        ),
        in_specs=[vm, vm],
        out_specs=(vm, vm),
        scratch_shapes=[
            pltpu.VMEM((nb, ns, r, 128), BF16),
            pltpu.VMEM((ns, r, 128), BF16),
            pltpu.VMEM((ns, r, 128), BF16),
            pltpu.VMEM((nb, ns, r, 128), BF16),
            pltpu.VMEM((nb, 32, 128), F32),
            pltpu.VMEM((32, 128), F32),
            pltpu.VMEM((ns, 32, 128), F32),
            pltpu.SemaphoreType.DMA((2, nb - 1)),
            pltpu.SemaphoreType.DMA((2, ns - 1)),
            pltpu.SemaphoreType.DMA((2, ns - 1)),
            pltpu.SemaphoreType.DMA((2, nb - 1)),
            pltpu.SemaphoreType.DMA((2, nb - 1)),
            pltpu.SemaphoreType.DMA((2, ns - 1)),
        ],
        compiler_params=pltpu.CompilerParams(
            collective_id=1, has_side_effects=True, vmem_limit_bytes=VMEM_LIMIT
        ),
        name="reduce",
    )(gwa.reshape(nb, ns, r, 128), small)
    grad_in = gin.transpose(1, 0, 2)[None, :, None]
    return (grad_in, grad_wa, osmall[27, :c1], osmall[:27, :c1].T, osmall[28, :1])


def solution(mesh):
    return jax.shard_map(
        functools.partial(body, mesh.shape["batch"], mesh.shape["slab"]),
        mesh=mesh,
        in_specs=(
            P("batch", None, "slab", None, None),
            P("batch", "slab", None),
            P("batch"),
            P("batch"),
            P(),
            P(),
            P(),
        ),
        out_specs=(P("batch", None, "slab", None, None), P(), P(), P(), P()),
        check_vma=False,
    )
```

time: 589 us -> 69.4 us (0.12)
  local copies, waits for them, and re-layouts: 309 us -> 9.93 us
  waiting for transfers between devices: 122 us -> 0 us
  blocking collectives: 59 us -> 0 us
  Pallas kernels: 0 us -> 56.3 us
  matrix products: 43.9 us -> 0 us
  other arithmetic: 24.9 us -> 0.59 us
  between operations: 18.9 us -> 2.13 us
  starting transfers between devices: 7.94 us -> 0 us
    slice x72 -> x1, local copies, waits for them, and re-layouts: 194 us -> 1.19 us  [body(): osmall[28, :1]]
    psum x1 -> x0, waiting for transfers between devices: 122 us -> none  [body(): sums = lax.psum((grad_wa, grad_ba, grad_wb, grad_bb), ('batch', 'slab'))]
    unnamed x185 -> x10, local copies, waits for them, and re-layouts: 86.9 us -> 5.35 us
    pallas_call x0 -> x3, Pallas kernels: none -> 56.3 us  [the longest x1 25.9 us: body(): pl.pallas_call(functools.partial(reduce_kernel, nb, ns, scale), out_shape...]
    dot_general x69 -> x0, matrix products: 43.9 us -> none  [the longest x64 26.8 us: transposed_forward(): jnp.dot(matrix.T, block, preferred_element_type=jnp.float32)]
    psum x1 -> x0, blocking collectives: 43.1 us -> none  [body(): sums = lax.psum((grad_wa, grad_ba, grad_wb, grad_bb), ('batch', 'slab'))]
    another operation x32 -> x4, local copies, waits for them, and re-layouts: 21 us -> 1.4 us  [the longest x2 0.76 us: body(): wbt = jnp.tile(weight_b.astype(F32).T, (1, 16))]
    all_gather x1 -> x0, blocking collectives: 15.9 us -> none  [body(): rows_block = lax.all_gather(grad_image, 'slab', axis=1, tiled=True)]
  transfers between devices with their start and end apart: 5 -> 0, of which waited for: 1 -> 0; matrix products, arithmetic and copies ran while one was open for 6% -> 0% of each run, Pallas kernels for 0% -> 0%
where the time goes in v1:
time: 69.4 us; the launch traced here: 69 us
  Pallas kernels  56.3 us (81%)
  local copies, waits for them, and re-layouts  9.93 us (14%)
  between operations  2.13 us (3%)
    pallas_call x1, Pallas kernels, body(): pl.pallas_call(functools.partial(reduce_kernel, nb, ns, scale), out_shape...  25.9 us
    pallas_call x1, Pallas kernels, body(): pl.pallas_call(functools.partial(local_kernel, ns), out_shape=(jax.ShapeD...  16.8 us
    pallas_call x1, Pallas kernels, body(): pl.pallas_call(functools.partial(gather_kernel, ns), out_shape=(jax.Shape...  13.6 us
    unnamed x10, local copies, waits for them, and re-layouts  5.35 us

profile of v1, /device:TPU:0, one launch (start us, length us, event | category | flops | bytes accessed | tf_op | source)
XLA Modules:
  0.0 69.0 jit_solution(3667639512352648967)
XLA Ops:
  1.9 0.0 copy-start.2
  2.0 0.0 copy-start.1
  2.1 0.6 pad_maximum_fusion.trig_ref
  2.7 0.0 copy-done.2
  2.7 0.6 broadcast_in_dim_tile.3.bias_ref
  3.3 0.0 copy-done.1
  3.3 0.1 copy.13
  3.4 0.0 copy-start
  3.5 0.7 %tile.8.wbt_ref = f32[27,512]{1,0:T(8,128)} reshape(f32[27,16,32]{2,1,0:T(8,128)S(1)} %tile.7) | data formatting | bytes 110592 | tf_op jit(solution)/shard_map/tile | solution.py:435
  4.2 0.2 copy-done
  4.4 0.8 %copy.17 = bf16[1,64,1,16,128]{4,1,3,2,0:T(8,128)(2,1)} copy(bf16[1,64,1,16,128]{4,3,2,1,0:T(8,128)(2,1)S(1)} %copy-done) | data formatting | bytes 524288 | tf_op args[0]
  5.2 13.6 %gather.1 = (bf16[2,16,64,128]{3,2,1,0:T(8,128)(2,1)}, bf16[8,32,256]{2,1,0:T(8,128)(2,1)}) custom-call(bf16[16,64,128]{2,1,0:T(8,128)(2,1)} %bitcast.18, bf16[32,256]{1,0:T(8,128)(2,1)} %bitcast.23), custom_call_target="tpu_custom_call" | custom-call | tf_op jit(solution)/shard_map/gather/pallas_call | solution.py:413
  18.7 16.8 %local.1 = (bf16[16,64,128]{2,1,0:T(8,128)(2,1)}, bf16[16,64,128]{2,1,0:T(8,128)(2,1)}, f32[32,128]{1,0:T(8,128)}) custom-call(f32[3]{0:T(128)} %pad_maximum_fusion.trig_ref, bf16[16,64,128]{2,1,0:T(8,128)(2,1)} %bitcast.19, bf16[2,16,64,128]{3,2,1,0:T(8,128)(2,1)} %get-tuple-element.12.halo_ref, bf16[256,256]{1,0:T(8,128)(2,1)} %bitcast.22, ...), custom_call_target="tpu_custom_call" | custom-call | tf_op jit(solution)/shard_map/local/pallas_call | solution.py:436
  35.6 1.8 %copy.14 = bf16[1,64,1,16,128]{4,3,2,1,0:T(8,128)(2,1)} copy(bf16[1,64,1,16,128]{4,1,3,2,0:T(8,128)(2,1)} %bitcast.21) | data formatting | bytes 524288
  37.4 25.9 %reduce.1 = (f32[64,2048]{1,0:T(8,128)}, f32[32,128]{1,0:T(8,128)}) custom-call(bf16[4,8,32,128]{3,2,1,0:T(8,128)(2,1)} %bitcast.20, f32[32,128]{1,0:T(8,128)} %get-tuple-element.16.small_ref), custom_call_target="tpu_custom_call" | custom-call | tf_op jit(solution)/shard_map/reduce/pallas_call | solution.py:461
  63.3 1.2 %slice.11 = f32[1,1]{1,0:T(1,128)} slice(f32[32,128]{1,0:T(8,128)} %get-tuple-element.18), slice={[28:29], [0:1]} | slice | bytes 8 | tf_op jit(solution)/shard_map/slice | solution.py:490
  64.5 1.2 %slice_bitcast_fusion.1 = f32[32]{0:T(128)} fusion(f32[32,128]{1,0:T(8,128)} %get-tuple-element.18), kind=kLoop, calls=%fused_computation.4 | loop fusion | bytes 256 | tf_op jit(solution)/shard_map/squeeze | solution.py:490
  65.7 0.7 %slice_bitcast_fusion = f32[32,27]{0,1:T(8,128)S(1)} fusion(f32[32,128]{1,0:T(8,128)} %get-tuple-element.18), kind=kLoop, calls=%fused_computation.2 | loop fusion | bytes 6912 | tf_op jit(solution)/shard_map/transpose | solution.py:490
  66.4 0.7 copy.15
  67.1 1.9 %copy.21 = f32[64,2048]{1,0:T(8,128)} copy(f32[64,2048]{1,0:T(8,128)} %get-tuple-element.30) | data formatting | bytes 1048576
  (3 shorter events, 0.0 us)
Async XLA Ops:
  1.9 0.8 %copy-start.2 = (f32[32]{0:T(128)S(1)}, f32[32]{0:T(128)}, u32[]{:S(2)}) copy-start(f32[32]{0:T(128)} %param.12) | copy-start | bytes 388
  2.0 1.3 %copy-start.1 = (bf16[32,27]{1,0:T(8,128)(2,1)S(1)}, bf16[32,27]{1,0:T(8,128)(2,1)}, u32[]{:S(2)}) copy-start(bf16[32,27]{1,0:T(8,128)(2,1)} %param.13) | copy-start | bytes 5188
  3.4 1.0 %copy-start = (bf16[1,64,1,16,128]{4,3,2,1,0:T(8,128)(2,1)S(1)}, bf16[1,64,1,16,128]{4,3,2,1,0:T(8,128)(2,1)}, u32[]{:S(2)}) copy-start(bf16[1,64,1,16,128]{4,3,2,1,0:T(8,128)(2,1)} %param.7) | copy-start | bytes 786436

commit v2 on v1

--- a/solution.py
+++ b/solution.py
@@ -105,7 +105,7 @@
     img_ref,
     wa_ref,
     bias_ref,
-    wbt_ref,
+    taps_ref,
     gin_ref,
     gwa_ref,
     small_ref,
@@ -177,9 +177,12 @@
     index = jnp.where(ok, 9 * az + 3 * by + cx, -1)
     inside = ((tz > 0) | (me > 0)) & ((tz < 3) | (me < ns - 1))
     masked_index = jnp.where(inside, index, -1)
+    spread = (iota((c1, 512), 0) == (iota((c1, 512), 1) & 31)).astype(F32).astype(BF16)
+    eye_t = (iota((27, 27), 0) == iota((27, 27), 1)).astype(F32).astype(BF16)
+    wbt = mm(nt_dot(eye_t, taps_ref[...]).astype(BF16), spread)
     wb_mat = jnp.zeros((96, 512), F32)
     for t in range(27):
-        wb_mat = jnp.where(masked_index == t, wbt_ref[t : t + 1, :], wb_mat)
+        wb_mat = jnp.where(masked_index == t, wbt[t : t + 1, :], wb_mat)
     wb_mat = wb_mat.astype(BF16)
     wb_ref[0:96, :] = wb_mat
     wb_ref[96:192, :] = wb_mat
@@ -237,7 +240,7 @@
             ga_ref[kx, py, pos + 128 : pos + 256, :] = zpad
     step = 512
     xc_id = iota((step, 128), 0) & 127
-    bias = bias_ref[...]
+    bias = jnp.concatenate([bias_ref[...]] * 8, axis=1)
 
     def forward(it, sums):
         start = pl.multiple_of(it * step, step)
@@ -289,7 +292,11 @@
     fold = packed[:, 0:128] + packed[:, 128:256] + packed[:, 256:384] + packed[:, 384:512]
     fold = fold + pltpu.roll(fold, 64, 1)
     fold = fold + pltpu.roll(fold, 32, 1)
-    small_ref[...] = fold
+    group = iota((8, 128), 1) >> 5
+    tight = fold[0:8]
+    for k in range(1, 4):
+        tight = jnp.where(group == k, fold[8 * k : 8 * k + 8], tight)
+    small_ref[...] = tight
 
     ky_src = ((1, 0), (0, 1), (1, 1), (0, 2))
 
@@ -321,8 +328,8 @@
 
 
 def reduce_kernel(
-    nb, ns, scale, part_ref, small_ref, out_ref, osmall_ref,
-    rb, mid, rs, full, srb, smid, srs, sems_b, sems_s, sems_g, sems_h, sems_x, sems_y,
+    nb, ns, part_ref, small_ref, full, osmall_ref,
+    rb, mid, rs, srb, smid, srs, sems_b, sems_s, sems_g, sems_h, sems_x, sems_y,
 ):
     mb = lax.axis_index("batch")
     me = lax.axis_index("slab")
@@ -375,7 +382,7 @@
     for s in range(1, ns):
         acc = acc + rs[s].astype(F32)
         sacc = sacc + srs[s]
-    osmall_ref[...] = sacc * scale
+    osmall_ref[...] = sacc
     full[mb, me] = acc.astype(BF16)
     third = []
     for d in range(1, ns):
@@ -389,17 +396,32 @@
         fourth.append(send(full.at[mb], full.at[mb], sems_h, d, (to, me)))
     for copy in fourth:
         copy.wait()
+
+
+def finish_kernel(scale, full_ref, osmall_ref, out_ref, ba_ref, wb_ref, bb_ref):
     c0 = out_ref.shape[0]
-    per = ns // 4
+    per = full_ref.shape[1] // 4
     for ky in range(4):
         groups = [
-            full[ky, kx * per : (kx + 1) * per].astype(F32).reshape(c0, 128) * scale
+            full_ref[ky, kx * per : (kx + 1) * per].astype(F32).reshape(c0, 128) * scale
             for kx in range(4)
         ]
         for kz in range(4):
             out_ref[:, kz * 512 + ky * 128 : kz * 512 + (ky + 1) * 128] = jnp.concatenate(
                 [g[:, kz * 32 : (kz + 1) * 32] for g in groups], axis=1
             )
+    tight = osmall_ref[...] * scale
+    table = jnp.concatenate([tight[:, k * 32 : (k + 1) * 32] for k in range(4)], axis=0)
+    eye = (
+        lax.broadcasted_iota(jnp.int32, (32, 32), 0) == lax.broadcasted_iota(jnp.int32, (32, 32), 1)
+    ).astype(F32)
+    flipped = lax.dot_general(
+        eye, table, (((1,), (1,)), ((), ())), precision=lax.Precision.HIGHEST,
+        preferred_element_type=F32,
+    )
+    wb_ref[...] = flipped[:, 0:27]
+    ba_ref[...] = table[27:28, :]
+    bb_ref[...] = table[28:29, 0:1]
 
 
 def body(nb, ns, activations, grad_image, pose_bin, shift, weight_a, bias_a, weight_b):
@@ -431,14 +453,12 @@
     )(x, img)
     angle = (pose_bin[0].astype(F32) + 0.5) * (math.pi / NBINS)
     trig = jnp.stack([jnp.cos(angle), jnp.sin(angle), shift[0].astype(F32)])
-    bias_t = jnp.tile(bias_a, 8)[None]
-    wbt = jnp.tile(weight_b.astype(F32).T, (1, 16))
     gin, gwa, small = pl.pallas_call(
         functools.partial(local_kernel, ns),
         out_shape=(
             jax.ShapeDtypeStruct((yc_n, c0, xc_n), BF16),
             jax.ShapeDtypeStruct((16, c0, 128), BF16),
-            jax.ShapeDtypeStruct((32, 128), F32),
+            jax.ShapeDtypeStruct((8, 128), F32),
         ),
         in_specs=[pl.BlockSpec(memory_space=pltpu.SMEM)] + [vm] * 6,
         out_specs=(vm, vm, vm),
@@ -454,15 +474,15 @@
         ],
         compiler_params=pltpu.CompilerParams(vmem_limit_bytes=VMEM_LIMIT),
         name="local",
-    )(trig, x, halo, gathered.reshape(ns * local_rows, width), weight_a, bias_t, wbt)
+    )(trig, x, halo, gathered.reshape(ns * local_rows, width), weight_a, bias_a.reshape(1, c1), weight_b)
     r = 256 // ns
     total_cells = nb * 2 * ns * 2 * yc_n * 2 * xc_n
     scale = 1.0 / math.sqrt(total_cells)
-    grad_wa, osmall = pl.pallas_call(
-        functools.partial(reduce_kernel, nb, ns, scale),
+    full, osmall = pl.pallas_call(
+        functools.partial(reduce_kernel, nb, ns),
         out_shape=(
-            jax.ShapeDtypeStruct(weight_a.shape, F32),
-            jax.ShapeDtypeStruct((32, 128), F32),
+            jax.ShapeDtypeStruct((nb, ns, r, 128), BF16),
+            jax.ShapeDtypeStruct((8, 128), F32),
         ),
         in_specs=[vm, vm],
         out_specs=(vm, vm),
@@ -470,10 +490,9 @@
             pltpu.VMEM((nb, ns, r, 128), BF16),
             pltpu.VMEM((ns, r, 128), BF16),
             pltpu.VMEM((ns, r, 128), BF16),
-            pltpu.VMEM((nb, ns, r, 128), BF16),
-            pltpu.VMEM((nb, 32, 128), F32),
-            pltpu.VMEM((32, 128), F32),
-            pltpu.VMEM((ns, 32, 128), F32),
+            pltpu.VMEM((nb, 8, 128), F32),
+            pltpu.VMEM((8, 128), F32),
+            pltpu.VMEM((ns, 8, 128), F32),
             pltpu.SemaphoreType.DMA((2, nb - 1)),
             pltpu.SemaphoreType.DMA((2, ns - 1)),
             pltpu.SemaphoreType.DMA((2, ns - 1)),
@@ -487,7 +506,20 @@
         name="reduce",
     )(gwa.reshape(nb, ns, r, 128), small)
     grad_in = gin.transpose(1, 0, 2)[None, :, None]
-    return (grad_in, grad_wa, osmall[27, :c1], osmall[:27, :c1].T, osmall[28, :1])
+    grad_wa, grad_ba, grad_wb, grad_bb = pl.pallas_call(
+        functools.partial(finish_kernel, scale),
+        out_shape=(
+            jax.ShapeDtypeStruct(weight_a.shape, F32),
+            jax.ShapeDtypeStruct((1, c1), F32),
+            jax.ShapeDtypeStruct(weight_b.shape, F32),
+            jax.ShapeDtypeStruct((1, 1), F32),
+        ),
+        in_specs=[vm, vm],
+        out_specs=(vm, vm, vm, vm),
+        compiler_params=pltpu.CompilerParams(vmem_limit_bytes=VMEM_LIMIT),
+        name="finish",
+    )(full, osmall)
+    return (grad_in, grad_wa, grad_ba.reshape(c1), grad_wb, grad_bb.reshape(1))
 
 
 def solution(mesh):

time: 69.4 us -> 62.6 us (0.902)
  local copies, waits for them, and re-layouts: 9.93 us -> 3.55 us
    unnamed x10 -> x2, local copies, waits for them, and re-layouts: 5.35 us -> 3.55 us
    another operation x4 -> x0, local copies, waits for them, and re-layouts: 1.4 us -> none  [the longest x2 0.76 us: body(): wbt = jnp.tile(weight_b.astype(F32).T, (1, 16))]
    slice x1 -> x0, local copies, waits for them, and re-layouts: 1.19 us -> none  [body(): osmall[28, :1]]
    squeeze x1 -> x0, local copies, waits for them, and re-layouts: 1.19 us -> none  [body(): osmall[27, :c1]]
    transpose x2 -> x0, local copies, waits for them, and re-layouts: 0.8 us -> none  [the longest x1 0.72 us: body(): osmall[:27, :c1]]
    pallas_call x1 -> x2, Pallas kernels: 25.9 us -> 25.9 us  [the longest x1 23.7 us: body(): pl.pallas_call(functools.partial(reduce_kernel, nb, ns), out_shape=(jax.S...]
where the time goes in v2:
time: 62.6 us; the launch traced here: 62.3 us
  Pallas kernels  56.1 us (90%)
  local copies, waits for them, and re-layouts  3.55 us (6%)
  between operations  2.1 us (3%)
    pallas_call x1, Pallas kernels, body(): pl.pallas_call(functools.partial(reduce_kernel, nb, ns), out_shape=(jax.S...  23.7 us
    pallas_call x1, Pallas kernels, body(): pl.pallas_call(functools.partial(local_kernel, ns), out_shape=(jax.ShapeD...  16.6 us
    pallas_call x1, Pallas kernels, body(): pl.pallas_call(functools.partial(gather_kernel, ns), out_shape=(jax.Shape...  13.6 us
    unnamed x2, local copies, waits for them, and re-layouts  3.55 us
    pallas_call x1, Pallas kernels, body(): pl.pallas_call(functools.partial(finish_kernel, scale), out_shape=(jax.Sh...  2.23 us

profile of v2, /device:TPU:0, one launch (start us, length us, event | category | flops | bytes accessed | tf_op | source)
XLA Modules:
  0.0 62.3 jit_solution(4135200277672763707)
XLA Ops:
  2.1 0.6 pad_maximum_fusion.trig_ref
  2.7 1.7 %copy.15 = bf16[1,64,1,16,128]{4,1,3,2,0:T(8,128)(2,1)} copy(bf16[1,64,1,16,128]{4,3,2,1,0:T(8,128)(2,1)} %param.7) | data formatting | bytes 524288 | tf_op args[0]
  4.4 13.6 %gather.1 = (bf16[2,16,64,128]{3,2,1,0:T(8,128)(2,1)}, bf16[8,32,256]{2,1,0:T(8,128)(2,1)}) custom-call(bf16[16,64,128]{2,1,0:T(8,128)(2,1)} %bitcast.14, bf16[32,256]{1,0:T(8,128)(2,1)} %bitcast.19), custom_call_target="tpu_custom_call" | custom-call | tf_op jit(solution)/shard_map/gather/pallas_call | solution.py:435
  17.9 16.6 %local.1 = (bf16[16,64,128]{2,1,0:T(8,128)(2,1)}, bf16[16,64,128]{2,1,0:T(8,128)(2,1)}, f32[8,128]{1,0:T(8,128)}) custom-call(f32[3]{0:T(128)} %pad_maximum_fusion.trig_ref, bf16[16,64,128]{2,1,0:T(8,128)(2,1)} %bitcast.15, bf16[2,16,64,128]{3,2,1,0:T(8,128)(2,1)} %get-tuple-element.16.halo_ref, bf16[256,256]{1,0:T(8,128)(2,1)} %bitcast.18, ...), custom_call_target="tpu_custom_call" | custom-call | tf_op jit(solution)/shard_map/local/pallas_call | solution.py:456
  34.5 1.8 %copy.13 = bf16[1,64,1,16,128]{4,3,2,1,0:T(8,128)(2,1)} copy(bf16[1,64,1,16,128]{4,1,3,2,0:T(8,128)(2,1)} %bitcast.17) | data formatting | bytes 524288
  36.4 23.7 %reduce.1 = (bf16[4,8,32,128]{3,2,1,0:T(8,128)(2,1)}, f32[8,128]{1,0:T(8,128)}) custom-call(bf16[4,8,32,128]{3,2,1,0:T(8,128)(2,1)} %bitcast.16, f32[8,128]{1,0:T(8,128)} %get-tuple-element.20.small_ref), custom_call_target="tpu_custom_call" | custom-call | tf_op jit(solution)/shard_map/reduce/pallas_call | solution.py:481
  60.1 2.2 %finish.1 = (f32[64,2048]{1,0:T(8,128)}, f32[1,32]{1,0:T(1,128)}, f32[32,27]{1,0:T(8,128)}, f32[1,1]{1,0:T(1,128)}) custom-call(bf16[4,8,32,128]{3,2,1,0:T(8,128)(2,1)} %get-tuple-element.21.full_ref, f32[8,128]{1,0:T(8,128)} %get-tuple-element.22.osmall_ref), custom_call_target="tpu_custom_call" | custom-call | tf_op jit(solution)/shard_map/finish/pallas_call | solution.py:509

commit v3 on v2

--- a/solution.py
+++ b/solution.py
@@ -98,6 +98,7 @@
 
 
 def local_kernel(
+    nb,
     ns,
     trig_ref,
     x_ref,
@@ -107,8 +108,8 @@
     bias_ref,
     taps_ref,
     gin_ref,
-    gwa_ref,
-    small_ref,
+    full,
+    osmall_ref,
     tt_ref,
     g_ref,
     gt_ref,
@@ -117,8 +118,53 @@
     w4_ref,
     wb_ref,
     act_ref,
+    part,
+    r0,
+    m0,
+    rb,
+    mid,
+    rs,
+    sr0,
+    sm0,
+    srb,
+    smid,
+    srs,
+    sems_c,
+    sems_b,
+    sems_z,
+    sems_gz,
+    sems_gb,
+    sems_gc,
+    sems_sc,
+    sems_sb,
+    sems_sz,
 ):
+    mb = lax.axis_index("batch")
     me = lax.axis_index("slab")
+    nh = ns // 2
+    core = lax.rem(me, 2)
+    hs = me // 2
+    partner = (mb, me + 1 - 2 * core)
+    barrier = pltpu.get_barrier_semaphore()
+    pl.semaphore_signal(barrier, inc=1, device_id=partner, device_id_type=MESH)
+    for d in range(1, nb):
+        pl.semaphore_signal(barrier, inc=1, device_id=(lax.rem(mb + d, nb), me), device_id_type=MESH)
+    for d in range(1, nh):
+        peer = (mb, 2 * lax.rem(hs + d, nh) + core)
+        pl.semaphore_signal(barrier, inc=1, device_id=peer, device_id_type=MESH)
+
+    def send(src, dst, sems, d, device):
+        copy = pltpu.make_async_remote_copy(
+            src_ref=src,
+            dst_ref=dst,
+            send_sem=sems.at[0, d - 1],
+            recv_sem=sems.at[1, d - 1],
+            device_id=device,
+            device_id_type=MESH,
+        )
+        copy.start()
+        return copy
+
     yc_n, c0, xc_n = x_ref.shape
     c1 = 32
     rows = img_ref.shape[0]
@@ -296,7 +342,7 @@
     tight = fold[0:8]
     for k in range(1, 4):
         tight = jnp.where(group == k, fold[8 * k : 8 * k + 8], tight)
-    small_ref[...] = tight
+    sr0[core] = tight
 
     ky_src = ((1, 0), (0, 1), (1, 1), (0, 2))
 
@@ -318,47 +364,35 @@
             gin_ref[it * (step // 128) + k] = flipped[:, k * 128 : (k + 1) * 128]
         return carry
 
-    lax.fori_loop(0, pos // step, backward, 0)
     xt = jnp.concatenate([x_ref[yc] for yc in range(yc_n)], axis=1)
+    per, r = part.shape[2] // 2, part.shape[3]
     for pair in range(8):
         s = jnp.concatenate([patch(2 * pair, 0, pos), patch(2 * pair + 1, 0, pos)], axis=1)
-        res = mm(xt, s).astype(BF16)
-        gwa_ref[2 * pair] = res[:, :128]
-        gwa_ref[2 * pair + 1] = res[:, 128:]
-
-
-def reduce_kernel(
-    nb, ns, part_ref, small_ref, full, osmall_ref,
-    rb, mid, rs, srb, smid, srs, sems_b, sems_s, sems_g, sems_h, sems_x, sems_y,
-):
-    mb = lax.axis_index("batch")
-    me = lax.axis_index("slab")
-    barrier = pltpu.get_barrier_semaphore()
-    for d in range(1, nb):
-        pl.semaphore_signal(barrier, inc=1, device_id=(lax.rem(mb + d, nb), me), device_id_type=MESH)
-    for d in range(1, ns):
-        pl.semaphore_signal(barrier, inc=1, device_id=(mb, lax.rem(me + d, ns)), device_id_type=MESH)
-    pl.semaphore_wait(barrier, nb + ns - 2)
-
-    def send(src, dst, sems, d, device):
-        copy = pltpu.make_async_remote_copy(
-            src_ref=src,
-            dst_ref=dst,
-            send_sem=sems.at[0, d - 1],
-            recv_sem=sems.at[1, d - 1],
-            device_id=device,
-            device_id_type=MESH,
-        )
-        copy.start()
-        return copy
-
+        res = mm(xt, s)
+        for h in range(2):
+            part[pair // 4, pair % 4, h * per : (h + 1) * per] = (
+                res[:, h * 128 : (h + 1) * 128].reshape(per, r, 128).astype(BF16)
+            )
+
+    pl.semaphore_wait(barrier, nb + nh - 1)
+    pair_copies = [
+        send(part.at[1 - core], r0, sems_c, 1, partner),
+        send(sr0.at[core], sr0.at[core], sems_sc, 1, partner),
+    ]
+    half = pos // step // 4
+    lax.fori_loop(0, half, backward, 0)
+    for copy in pair_copies:
+        copy.wait()
+    m0[...] = (part[core].astype(F32) + r0[...].astype(F32)).astype(BF16)
+    sm0[...] = sr0[0] + sr0[1]
     first = []
     for d in range(1, nb):
         to = lax.rem(mb + d, nb)
-        first.append(send(part_ref.at[to], rb.at[mb], sems_b, d, (to, me)))
-        first.append(send(small_ref, srb.at[mb], sems_x, d, (to, me)))
-    rb[mb] = part_ref[mb]
-    srb[mb] = small_ref[...]
+        first.append(send(m0.at[to], rb.at[mb], sems_b, d, (to, me)))
+        first.append(send(sm0, srb.at[mb], sems_sb, d, (to, me)))
+    rb[mb] = m0[mb]
+    srb[mb] = sm0[...]
+    lax.fori_loop(half, pos // step, backward, 0)
     for copy in first:
         copy.wait()
     acc = rb[0].astype(F32)
@@ -369,41 +403,45 @@
     mid[...] = acc.astype(BF16)
     smid[...] = sacc
     second = []
-    for d in range(1, ns):
-        to = lax.rem(me + d, ns)
-        second.append(send(mid.at[to], rs.at[me], sems_s, d, (mb, to)))
-        second.append(send(smid, srs.at[me], sems_y, d, (mb, to)))
-    rs[me] = mid[me]
-    srs[me] = sacc
+    for d in range(1, nh):
+        to = lax.rem(hs + d, nh)
+        second.append(send(mid.at[to], rs.at[hs], sems_z, d, (mb, 2 * to + core)))
+        second.append(send(smid, srs.at[hs], sems_sz, d, (mb, 2 * to + core)))
+    rs[hs] = mid[hs]
+    srs[hs] = sacc
     for copy in second:
         copy.wait()
     acc = rs[0].astype(F32)
     sacc = srs[0]
-    for s in range(1, ns):
-        acc = acc + rs[s].astype(F32)
-        sacc = sacc + srs[s]
+    for k in range(1, nh):
+        acc = acc + rs[k].astype(F32)
+        sacc = sacc + srs[k]
     osmall_ref[...] = sacc
-    full[mb, me] = acc.astype(BF16)
+    full[core, mb, hs] = acc.astype(BF16)
     third = []
-    for d in range(1, ns):
-        to = lax.rem(me + d, ns)
-        third.append(send(full.at[mb, me], full.at[mb, me], sems_g, d, (mb, to)))
+    for d in range(1, nh):
+        to = (mb, 2 * lax.rem(hs + d, nh) + core)
+        third.append(send(full.at[core, mb, hs], full.at[core, mb, hs], sems_gz, d, to))
     for copy in third:
         copy.wait()
     fourth = []
     for d in range(1, nb):
-        to = lax.rem(mb + d, nb)
-        fourth.append(send(full.at[mb], full.at[mb], sems_h, d, (to, me)))
+        to = (lax.rem(mb + d, nb), me)
+        fourth.append(send(full.at[core, mb], full.at[core, mb], sems_gb, d, to))
     for copy in fourth:
         copy.wait()
+    send(full.at[core], full.at[core], sems_gc, 1, partner).wait()
 
 
 def finish_kernel(scale, full_ref, osmall_ref, out_ref, ba_ref, wb_ref, bb_ref):
     c0 = out_ref.shape[0]
-    per = full_ref.shape[1] // 4
+    per = full_ref.shape[2] // 2
     for ky in range(4):
         groups = [
-            full_ref[ky, kx * per : (kx + 1) * per].astype(F32).reshape(c0, 128) * scale
+            full_ref[ky // 2, 2 * (ky % 2) + kx // 2, (kx % 2) * per : (kx % 2 + 1) * per]
+            .astype(F32)
+            .reshape(c0, 128)
+            * scale
             for kx in range(4)
         ]
         for kz in range(4):
@@ -453,11 +491,15 @@
     )(x, img)
     angle = (pose_bin[0].astype(F32) + 0.5) * (math.pi / NBINS)
     trig = jnp.stack([jnp.cos(angle), jnp.sin(angle), shift[0].astype(F32)])
-    gin, gwa, small = pl.pallas_call(
-        functools.partial(local_kernel, ns),
+    nh = ns // 2
+    r = 512 // (nb * nh)
+    total_cells = nb * 2 * ns * 2 * yc_n * 2 * xc_n
+    scale = 1.0 / math.sqrt(total_cells)
+    gin, full, osmall = pl.pallas_call(
+        functools.partial(local_kernel, nb, ns),
         out_shape=(
             jax.ShapeDtypeStruct((yc_n, c0, xc_n), BF16),
-            jax.ShapeDtypeStruct((16, c0, 128), BF16),
+            jax.ShapeDtypeStruct((2, nb, nh, r, 128), BF16),
             jax.ShapeDtypeStruct((8, 128), F32),
         ),
         in_specs=[pl.BlockSpec(memory_space=pltpu.SMEM)] + [vm] * 6,
@@ -471,40 +513,35 @@
             pltpu.VMEM((c0, 2048), BF16),
             pltpu.VMEM((192, 512), BF16),
             pltpu.VMEM((pos, 512), BF16),
-        ],
-        compiler_params=pltpu.CompilerParams(vmem_limit_bytes=VMEM_LIMIT),
-        name="local",
-    )(trig, x, halo, gathered.reshape(ns * local_rows, width), weight_a, bias_a.reshape(1, c1), weight_b)
-    r = 256 // ns
-    total_cells = nb * 2 * ns * 2 * yc_n * 2 * xc_n
-    scale = 1.0 / math.sqrt(total_cells)
-    full, osmall = pl.pallas_call(
-        functools.partial(reduce_kernel, nb, ns),
-        out_shape=(
-            jax.ShapeDtypeStruct((nb, ns, r, 128), BF16),
-            jax.ShapeDtypeStruct((8, 128), F32),
-        ),
-        in_specs=[vm, vm],
-        out_specs=(vm, vm),
-        scratch_shapes=[
-            pltpu.VMEM((nb, ns, r, 128), BF16),
-            pltpu.VMEM((ns, r, 128), BF16),
-            pltpu.VMEM((ns, r, 128), BF16),
+            pltpu.VMEM((2, nb, nh, r, 128), BF16),
+            pltpu.VMEM((nb, nh, r, 128), BF16),
+            pltpu.VMEM((nb, nh, r, 128), BF16),
+            pltpu.VMEM((nb, nh, r, 128), BF16),
+            pltpu.VMEM((nh, r, 128), BF16),
+            pltpu.VMEM((nh, r, 128), BF16),
+            pltpu.VMEM((2, 8, 128), F32),
+            pltpu.VMEM((8, 128), F32),
             pltpu.VMEM((nb, 8, 128), F32),
             pltpu.VMEM((8, 128), F32),
-            pltpu.VMEM((ns, 8, 128), F32),
+            pltpu.VMEM((nh, 8, 128), F32),
+            pltpu.SemaphoreType.DMA((2, 1)),
             pltpu.SemaphoreType.DMA((2, nb - 1)),
-            pltpu.SemaphoreType.DMA((2, ns - 1)),
-            pltpu.SemaphoreType.DMA((2, ns - 1)),
+            pltpu.SemaphoreType.DMA((2, nh - 1)),
+            pltpu.SemaphoreType.DMA((2, nh - 1)),
             pltpu.SemaphoreType.DMA((2, nb - 1)),
+            pltpu.SemaphoreType.DMA((2, 1)),
+            pltpu.SemaphoreType.DMA((2, 1)),
             pltpu.SemaphoreType.DMA((2, nb - 1)),
-            pltpu.SemaphoreType.DMA((2, ns - 1)),
+            pltpu.SemaphoreType.DMA((2, nh - 1)),
         ],
         compiler_params=pltpu.CompilerParams(
             collective_id=1, has_side_effects=True, vmem_limit_bytes=VMEM_LIMIT
         ),
-        name="reduce",
-    )(gwa.reshape(nb, ns, r, 128), small)
+        name="local",
+    )(
+        trig, x, halo, gathered.reshape(ns * local_rows, width), weight_a,
+        bias_a.reshape(1, c1), weight_b,
+    )
     grad_in = gin.transpose(1, 0, 2)[None, :, None]
     grad_wa, grad_ba, grad_wb, grad_bb = pl.pallas_call(
         functools.partial(finish_kernel, scale),

time: 62.6 us -> 53.2 us (0.85)
  Pallas kernels: 56.1 us -> 46.7 us
    pallas_call x2 -> x1, Pallas kernels: 40.3 us -> 30.9 us  [body(): pl.pallas_call(functools.partial(local_kernel, nb, ns), out_shape=(jax.Sh...]
where the time goes in v3:
time: 53.2 us; the launch traced here: 52.9 us
  Pallas kernels  46.7 us (88%)
  local copies, waits for them, and re-layouts  3.55 us (7%)
  between operations  2.1 us (4%)
  other arithmetic  0.59 us (1%)
    pallas_call x1, Pallas kernels, body(): pl.pallas_call(functools.partial(local_kernel, nb, ns), out_shape=(jax.Sh...  30.9 us
    pallas_call x1, Pallas kernels, body(): pl.pallas_call(functools.partial(gather_kernel, ns), out_shape=(jax.Shape...  13.6 us
    unnamed x2, local copies, waits for them, and re-layouts  3.55 us
    pallas_call x1, Pallas kernels, body(): pl.pallas_call(functools.partial(finish_kernel, scale), out_shape=(jax.Sh...  2.23 us

profile of v3, /device:TPU:0, one launch (start us, length us, event | category | flops | bytes accessed | tf_op | source)
XLA Modules:
  0.0 52.9 jit_solution(7743915968239571192)
XLA Ops:
  2.1 0.6 %pad_maximum_fusion.trig_ref = f32[3]{0:T(128)} fusion(f32[1]{0:T(128)S(6)} %convert_element_type.9, f32[1]{0:T(128)S(6)} %sin.4, f32[1]{0:T(128)S(6)} %cos.4), kind=kLoop, calls=%fused_computation.1 | loop fusion | flops 6 | bytes 24 | tf_op jit(solution)/shard_map/stack | solution.py:493
  2.7 1.7 %copy.15 = bf16[1,64,1,16,128]{4,1,3,2,0:T(8,128)(2,1)} copy(bf16[1,64,1,16,128]{4,3,2,1,0:T(8,128)(2,1)} %param.7) | data formatting | bytes 524288 | tf_op args[0]
  4.4 13.6 %gather.1 = (bf16[2,16,64,128]{3,2,1,0:T(8,128)(2,1)}, bf16[8,32,256]{2,1,0:T(8,128)(2,1)}) custom-call(bf16[16,64,128]{2,1,0:T(8,128)(2,1)} %bitcast.13, bf16[32,256]{1,0:T(8,128)(2,1)} %bitcast.17), custom_call_target="tpu_custom_call" | custom-call | tf_op jit(solution)/shard_map/gather/pallas_call | solution.py:473
  18.0 30.9 %local.1 = (bf16[16,64,128]{2,1,0:T(8,128)(2,1)}, bf16[2,4,4,32,128]{4,3,2,1,0:T(8,128)(2,1)}, f32[8,128]{1,0:T(8,128)}) custom-call(f32[3]{0:T(128)} %pad_maximum_fusion.trig_ref, bf16[16,64,128]{2,1,0:T(8,128)(2,1)} %bitcast.14, bf16[2,16,64,128]{3,2,1,0:T(8,128)(2,1)} %get-tuple-element.14.halo_ref, bf16[256,256]{1,0:T(8,128)(2,1)} %bitcast.16, ...), custom_call_target="tpu_custom_call" | custom-call | tf_op jit(solution)/shard_map/local/pallas_call | solution.py:498
  48.9 1.8 %copy.13 = bf16[1,64,1,16,128]{4,3,2,1,0:T(8,128)(2,1)} copy(bf16[1,64,1,16,128]{4,1,3,2,0:T(8,128)(2,1)} %bitcast.15) | data formatting | bytes 524288
  50.7 2.2 %finish.1 = (f32[64,2048]{1,0:T(8,128)}, f32[1,32]{1,0:T(1,128)}, f32[32,27]{1,0:T(8,128)}, f32[1,1]{1,0:T(1,128)}) custom-call(bf16[2,4,4,32,128]{4,3,2,1,0:T(8,128)(2,1)} %get-tuple-element.17.full_ref, f32[8,128]{1,0:T(8,128)} %get-tuple-element.18.osmall_ref), custom_call_target="tpu_custom_call" | custom-call | tf_op jit(solution)/shard_map/finish/pallas_call | solution.py:546

commit v4 on v3

--- a/solution.py
+++ b/solution.py
@@ -23,86 +23,11 @@
     return jnp.dot(a, b, preferred_element_type=F32)
 
 
-def gather_kernel(ns, x_ref, img_ref, halo_ref, all_ref, h_send, h_recv, g_send, g_recv):
-    mb = lax.axis_index("batch")
-    me = lax.axis_index("slab")
-    barrier = pltpu.get_barrier_semaphore()
-    for d in range(1, ns):
-        pl.semaphore_signal(
-            barrier, inc=1, device_id=(mb, lax.rem(me + d, ns)), device_id_type=MESH
-        )
-    pl.semaphore_wait(barrier, ns - 1)
-
-    def to_right():
-        return pltpu.make_async_remote_copy(
-            src_ref=x_ref,
-            dst_ref=halo_ref.at[0],
-            send_sem=h_send.at[0],
-            recv_sem=h_recv.at[0],
-            device_id=(mb, lax.rem(me + 1, ns)),
-            device_id_type=MESH,
-        )
-
-    def to_left():
-        return pltpu.make_async_remote_copy(
-            src_ref=x_ref,
-            dst_ref=halo_ref.at[1],
-            send_sem=h_send.at[1],
-            recv_sem=h_recv.at[1],
-            device_id=(mb, lax.rem(me + ns - 1, ns)),
-            device_id_type=MESH,
-        )
-
-    @pl.when(me < ns - 1)
-    def _():
-        to_right().start()
-
-    @pl.when(me > 0)
-    def _():
-        to_left().start()
-
-    copies = []
-    for d in range(1, ns):
-        copy = pltpu.make_async_remote_copy(
-            src_ref=img_ref,
-            dst_ref=all_ref.at[me],
-            send_sem=g_send.at[d - 1],
-            recv_sem=g_recv.at[d - 1],
-            device_id=(mb, lax.rem(me + d, ns)),
-            device_id_type=MESH,
-        )
-        copy.start()
-        copies.append(copy)
-    all_ref[me] = img_ref[...]
-
-    @pl.when(me == 0)
-    def _():
-        halo_ref[0] = jnp.zeros(halo_ref.shape[1:], halo_ref.dtype)
-
-    @pl.when(me == ns - 1)
-    def _():
-        halo_ref[1] = jnp.zeros(halo_ref.shape[1:], halo_ref.dtype)
-
-    for copy in copies:
-        copy.wait()
-
-    @pl.when(me < ns - 1)
-    def _():
-        to_right().wait_send()
-        to_left().wait_recv()
-
-    @pl.when(me > 0)
-    def _():
-        to_left().wait_send()
-        to_right().wait_recv()
-
-
 def local_kernel(
     nb,
     ns,
     trig_ref,
     x_ref,
-    halo_ref,
     img_ref,
     wa_ref,
     bias_ref,
@@ -118,6 +43,12 @@
     w4_ref,
     wb_ref,
     act_ref,
+    halo_ref,
+    all_ref,
+    h_send,
+    h_recv,
+    g_send,
+    g_recv,
     part,
     r0,
     m0,
@@ -146,12 +77,63 @@
     hs = me // 2
     partner = (mb, me + 1 - 2 * core)
     barrier = pltpu.get_barrier_semaphore()
-    pl.semaphore_signal(barrier, inc=1, device_id=partner, device_id_type=MESH)
     for d in range(1, nb):
         pl.semaphore_signal(barrier, inc=1, device_id=(lax.rem(mb + d, nb), me), device_id_type=MESH)
-    for d in range(1, nh):
-        peer = (mb, 2 * lax.rem(hs + d, nh) + core)
+    for d in range(1, ns):
+        peer = (mb, lax.rem(me + d, ns))
         pl.semaphore_signal(barrier, inc=1, device_id=peer, device_id_type=MESH)
+    pl.semaphore_wait(barrier, nb + ns - 2)
+
+    images = []
+    for d in range(1, ns):
+        copy = pltpu.make_async_remote_copy(
+            src_ref=img_ref,
+            dst_ref=all_ref.at[me],
+            send_sem=g_send.at[d - 1],
+            recv_sem=g_recv.at[d - 1],
+            device_id=(mb, lax.rem(me + d, ns)),
+            device_id_type=MESH,
+        )
+        copy.start()
+        images.append(copy)
+
+    def to_right():
+        return pltpu.make_async_remote_copy(
+            src_ref=x_ref,
+            dst_ref=halo_ref.at[0],
+            send_sem=h_send.at[0],
+            recv_sem=h_recv.at[0],
+            device_id=(mb, lax.rem(me + 1, ns)),
+            device_id_type=MESH,
+        )
+
+    def to_left():
+        return pltpu.make_async_remote_copy(
+            src_ref=x_ref,
+            dst_ref=halo_ref.at[1],
+            send_sem=h_send.at[1],
+            recv_sem=h_recv.at[1],
+            device_id=(mb, lax.rem(me + ns - 1, ns)),
+            device_id_type=MESH,
+        )
+
+    @pl.when(me < ns - 1)
+    def _():
+        to_right().start()
+
+    @pl.when(me > 0)
+    def _():
+        to_left().start()
+
+    all_ref[me] = img_ref[...]
+
+    @pl.when(me == 0)
+    def _():
+        halo_ref[0] = jnp.zeros(halo_ref.shape[1:], halo_ref.dtype)
+
+    @pl.when(me == ns - 1)
+    def _():
+        halo_ref[1] = jnp.zeros(halo_ref.shape[1:], halo_ref.dtype)
 
     def send(src, dst, sems, d, device):
         copy = pltpu.make_async_remote_copy(
@@ -167,7 +149,7 @@
 
     yc_n, c0, xc_n = x_ref.shape
     c1 = 32
-    rows = img_ref.shape[0]
+    rows = ns * img_ref.shape[0]
     depth = 2 * ns
     height = 2 * yc_n
     pos = yc_n * xc_n
@@ -237,7 +219,10 @@
     col_x = iota((width, 512), 1)
     fine = 2 * (col_x & 127) + (col_x >> 7) - 1
     sel = (iota((width, 512), 0) == fine).astype(F32).astype(BF16)
-    ims = mm(img_ref[...], sel).astype(BF16)
+    for copy in images:
+        copy.wait()
+    whole_image = all_ref[...].astype(F32).reshape(rows, width).astype(BF16)
+    ims = mm(whole_image, sel).astype(BF16)
     shape3 = (yc_n, 24, rows)
     j = iota(shape3, 1)
     y = 2 * iota(shape3, 0) + (j & 3) - 1
@@ -274,6 +259,18 @@
         gt = jnp.concatenate([bhi, blo], axis=0)
         gt_ref[yc] = gt
         g_ref[yc * 128 : (yc + 1) * 128, :] = nt_dot(eye, gt).astype(BF16)
+
+    @pl.when(me < ns - 1)
+    def _():
+        to_right().wait_send()
+        to_left().wait_recv()
+
+    @pl.when(me > 0)
+    def _():
+        to_left().wait_send()
+        to_right().wait_recv()
+
+    for yc in range(yc_n):
         planes = jnp.concatenate([halo_ref[0, yc], x_ref[yc], halo_ref[1, yc]], axis=0)
         r = nt_dot(shift_mat, planes).astype(BF16)
         for dxi in range(3):
@@ -374,7 +371,6 @@
                 res[:, h * 128 : (h + 1) * 128].reshape(per, r, 128).astype(BF16)
             )
 
-    pl.semaphore_wait(barrier, nb + nh - 1)
     pair_copies = [
         send(part.at[1 - core], r0, sems_c, 1, partner),
         send(sr0.at[core], sr0.at[core], sems_sc, 1, partner),
@@ -470,25 +466,6 @@
     x = activations[0, :, 0].transpose(1, 0, 2)
     img = grad_image[0]
     local_rows, width = img.shape
-    halo, gathered = pl.pallas_call(
-        functools.partial(gather_kernel, ns),
-        out_shape=(
-            jax.ShapeDtypeStruct((2,) + x.shape, BF16),
-            jax.ShapeDtypeStruct((ns, local_rows, width), BF16),
-        ),
-        in_specs=[vm, vm],
-        out_specs=(vm, vm),
-        scratch_shapes=[
-            pltpu.SemaphoreType.DMA((2,)),
-            pltpu.SemaphoreType.DMA((2,)),
-            pltpu.SemaphoreType.DMA((ns - 1,)),
-            pltpu.SemaphoreType.DMA((ns - 1,)),
-        ],
-        compiler_params=pltpu.CompilerParams(
-            collective_id=0, has_side_effects=True, vmem_limit_bytes=VMEM_LIMIT
-        ),
-        name="gather",
-    )(x, img)
     angle = (pose_bin[0].astype(F32) + 0.5) * (math.pi / NBINS)
     trig = jnp.stack([jnp.cos(angle), jnp.sin(angle), shift[0].astype(F32)])
     nh = ns // 2
@@ -502,7 +479,7 @@
             jax.ShapeDtypeStruct((2, nb, nh, r, 128), BF16),
             jax.ShapeDtypeStruct((8, 128), F32),
         ),
-        in_specs=[pl.BlockSpec(memory_space=pltpu.SMEM)] + [vm] * 6,
+        in_specs=[pl.BlockSpec(memory_space=pltpu.SMEM)] + [vm] * 5,
         out_specs=(vm, vm, vm),
         scratch_shapes=[
             pltpu.VMEM((3, pos + 256, 192), BF16),
@@ -513,6 +490,12 @@
             pltpu.VMEM((c0, 2048), BF16),
             pltpu.VMEM((192, 512), BF16),
             pltpu.VMEM((pos, 512), BF16),
+            pltpu.VMEM((2,) + x.shape, BF16),
+            pltpu.VMEM((ns, local_rows, width), BF16),
+            pltpu.SemaphoreType.DMA((2,)),
+            pltpu.SemaphoreType.DMA((2,)),
+            pltpu.SemaphoreType.DMA((ns - 1,)),
+            pltpu.SemaphoreType.DMA((ns - 1,)),
             pltpu.VMEM((2, nb, nh, r, 128), BF16),
             pltpu.VMEM((nb, nh, r, 128), BF16),
             pltpu.VMEM((nb, nh, r, 128), BF16),
@@ -535,11 +518,11 @@
             pltpu.SemaphoreType.DMA((2, nh - 1)),
         ],
         compiler_params=pltpu.CompilerParams(
-            collective_id=1, has_side_effects=True, vmem_limit_bytes=VMEM_LIMIT
+            collective_id=0, has_side_effects=True, vmem_limit_bytes=VMEM_LIMIT
         ),
         name="local",
     )(
-        trig, x, halo, gathered.reshape(ns * local_rows, width), weight_a,
+        trig, x, img, weight_a,
         bias_a.reshape(1, c1), weight_b,
     )
     grad_in = gin.transpose(1, 0, 2)[None, :, None]

time: 53.2 us -> 49.3 us (0.927)
  Pallas kernels: 46.7 us -> 42.9 us
    pallas_call x1 -> x0, Pallas kernels: 13.6 us -> none  [body(): pl.pallas_call(functools.partial(gather_kernel, ns), out_shape=(jax.Shape...]
    pallas_call x1, Pallas kernels: 30.9 us -> 40.6 us  [body(): pl.pallas_call(functools.partial(local_kernel, nb, ns), out_shape=(jax.Sh...]
where the time goes in v4:
time: 49.3 us; the launch traced here: 49.1 us
  Pallas kernels  42.9 us (87%)
  local copies, waits for them, and re-layouts  3.55 us (7%)
  between operations  2.09 us (4%)
  other arithmetic  0.59 us (1%)
    pallas_call x1, Pallas kernels, body(): pl.pallas_call(functools.partial(local_kernel, nb, ns), out_shape=(jax.Sh...  40.6 us
    unnamed x2, local copies, waits for them, and re-layouts  3.55 us
    pallas_call x1, Pallas kernels, body(): pl.pallas_call(functools.partial(finish_kernel, scale), out_shape=(jax.Sh...  2.23 us

profile of v4, /device:TPU:0, one launch (start us, length us, event | category | flops | bytes accessed | tf_op | source)
XLA Modules:
  0.0 49.1 jit_solution(3931019582385694342)
XLA Ops:
  2.1 0.6 %pad_maximum_fusion.trig_ref = f32[3]{0:T(128)} fusion(f32[1]{0:T(128)S(6)} %convert_element_type.9, f32[1]{0:T(128)S(6)} %sin.4, f32[1]{0:T(128)S(6)} %cos.4), kind=kLoop, calls=%fused_computation.1 | loop fusion | flops 6 | bytes 24 | tf_op jit(solution)/shard_map/stack | solution.py:470
  2.7 1.7 %copy.15 = bf16[1,64,1,16,128]{4,1,3,2,0:T(8,128)(2,1)} copy(bf16[1,64,1,16,128]{4,3,2,1,0:T(8,128)(2,1)} %param.7) | data formatting | bytes 524288 | tf_op args[0]
  4.4 40.6 %local.1 = (bf16[16,64,128]{2,1,0:T(8,128)(2,1)}, bf16[2,4,4,32,128]{4,3,2,1,0:T(8,128)(2,1)}, f32[8,128]{1,0:T(8,128)}) custom-call(f32[3]{0:T(128)} %pad_maximum_fusion.trig_ref, bf16[16,64,128]{2,1,0:T(8,128)(2,1)} %bitcast.12, bf16[32,256]{1,0:T(8,128)(2,1)} %bitcast.14, bf16[64,2048]{1,0:T(8,128)(2,1)} %wa_ref.1, f32[1,32]{1,0:T(1,128)} %bitcast.15, ...), custom_call_target="tpu_custom_call" | custom-call | tf_op jit(solution)/shard_map/local/pallas_call | solution.py:475
  45.0 1.8 %copy.13 = bf16[1,64,1,16,128]{4,3,2,1,0:T(8,128)(2,1)} copy(bf16[1,64,1,16,128]{4,1,3,2,0:T(8,128)(2,1)} %bitcast.13) | data formatting | bytes 524288
  46.9 2.2 %finish.1 = (f32[64,2048]{1,0:T(8,128)}, f32[1,32]{1,0:T(1,128)}, f32[32,27]{1,0:T(8,128)}, f32[1,1]{1,0:T(1,128)}) custom-call(bf16[2,4,4,32,128]{4,3,2,1,0:T(8,128)(2,1)} %get-tuple-element.13.full_ref, f32[8,128]{1,0:T(8,128)} %get-tuple-element.14.osmall_ref), custom_call_target="tpu_custom_call" | custom-call | tf_op jit(solution)/shard_map/finish/pallas_call | solution.py:529

commit v5 on v4

--- a/solution.py
+++ b/solution.py
@@ -424,9 +424,13 @@
     for d in range(1, nb):
         to = (lax.rem(mb + d, nb), me)
         fourth.append(send(full.at[core, mb], full.at[core, mb], sems_gb, d, to))
-    for copy in fourth:
+    fifth = [send(full.at[core, mb], full.at[core, mb], sems_gc, 1, partner)]
+    for d in range(1, nb):
+        fourth[d - 1].wait()
+        came = full.at[core, lax.rem(mb + nb - d, nb)]
+        fifth.append(send(came, came, sems_gc, d + 1, partner))
+    for copy in fifth:
         copy.wait()
-    send(full.at[core], full.at[core], sems_gc, 1, partner).wait()
 
 
 def finish_kernel(scale, full_ref, osmall_ref, out_ref, ba_ref, wb_ref, bb_ref):
@@ -512,7 +516,7 @@
             pltpu.SemaphoreType.DMA((2, nh - 1)),
             pltpu.SemaphoreType.DMA((2, nh - 1)),
             pltpu.SemaphoreType.DMA((2, nb - 1)),
-            pltpu.SemaphoreType.DMA((2, 1)),
+            pltpu.SemaphoreType.DMA((2, nb)),
             pltpu.SemaphoreType.DMA((2, 1)),
             pltpu.SemaphoreType.DMA((2, nb - 1)),
             pltpu.SemaphoreType.DMA((2, nh - 1)),

time: 49.3 us -> 49.3 us (level)
  no operation moved by 1% of the time
where the time goes in v5:
time: 49.3 us; the launch traced here: 49 us
  Pallas kernels  42.8 us (87%)
  local copies, waits for them, and re-layouts  3.55 us (7%)
  between operations  2.09 us (4%)
  other arithmetic  0.59 us (1%)
    pallas_call x1, Pallas kernels, body(): pl.pallas_call(functools.partial(local_kernel, nb, ns), out_shape=(jax.Sh...  40.6 us
    unnamed x2, local copies, waits for them, and re-layouts  3.55 us
    pallas_call x1, Pallas kernels, body(): pl.pallas_call(functools.partial(finish_kernel, scale), out_shape=(jax.Sh...  2.23 us

profile of v5, /device:TPU:0, one launch (start us, length us, event | category | flops | bytes accessed | tf_op | source)
XLA Modules:
  0.0 49.0 jit_solution(12474139036945085930)
XLA Ops:
  2.1 0.6 %pad_maximum_fusion.trig_ref = f32[3]{0:T(128)} fusion(f32[1]{0:T(128)S(6)} %convert_element_type.9, f32[1]{0:T(128)S(6)} %sin.4, f32[1]{0:T(128)S(6)} %cos.4), kind=kLoop, calls=%fused_computation.1 | loop fusion | flops 6 | bytes 24 | tf_op jit(solution)/shard_map/stack | solution.py:474
  2.7 1.7 %copy.15 = bf16[1,64,1,16,128]{4,1,3,2,0:T(8,128)(2,1)} copy(bf16[1,64,1,16,128]{4,3,2,1,0:T(8,128)(2,1)} %param.7) | data formatting | bytes 524288 | tf_op args[0]
  4.4 40.6 %local.1 = (bf16[16,64,128]{2,1,0:T(8,128)(2,1)}, bf16[2,4,4,32,128]{4,3,2,1,0:T(8,128)(2,1)}, f32[8,128]{1,0:T(8,128)}) custom-call(f32[3]{0:T(128)} %pad_maximum_fusion.trig_ref, bf16[16,64,128]{2,1,0:T(8,128)(2,1)} %bitcast.12, bf16[32,256]{1,0:T(8,128)(2,1)} %bitcast.14, bf16[64,2048]{1,0:T(8,128)(2,1)} %wa_ref.1, f32[1,32]{1,0:T(1,128)} %bitcast.15, ...), custom_call_target="tpu_custom_call" | custom-call | tf_op jit(solution)/shard_map/local/pallas_call | solution.py:479
  45.0 1.8 %copy.13 = bf16[1,64,1,16,128]{4,3,2,1,0:T(8,128)(2,1)} copy(bf16[1,64,1,16,128]{4,1,3,2,0:T(8,128)(2,1)} %bitcast.13) | data formatting | bytes 524288
  46.8 2.2 %finish.1 = (f32[64,2048]{1,0:T(8,128)}, f32[1,32]{1,0:T(1,128)}, f32[32,27]{1,0:T(8,128)}, f32[1,1]{1,0:T(1,128)}) custom-call(bf16[2,4,4,32,128]{4,3,2,1,0:T(8,128)(2,1)} %get-tuple-element.13.full_ref, f32[8,128]{1,0:T(8,128)} %get-tuple-element.14.osmall_ref), custom_call_target="tpu_custom_call" | custom-call | tf_op jit(solution)/shard_map/finish/pallas_call | solution.py:533
